TPU v7x, 32 devices: a whole 2x2x4 slice. The times are simulated.
32 devices in a mesh: space: 8 (over z, core), chaos: 4 (over y, x).
Axes of the slice: x: 2, y: 2, z: 4, core: 2. Of those that a mesh axis runs over, the one named last changes fastest.
Arguments:
- chaos_modes: float32 [84, 32768], P(None, ('space', 'chaos')), may hold values from -0.2 to 0.2
- newton_heading: float32 [84, 32768], P(None, ('space', 'chaos')), may hold values from -0.2 to 0.2
- source: float32 [32768], P(('space', 'chaos')), may hold values from -6 to 6
- nodes: float32 [512, 6], replicated, may hold values from -3 to 3
- weights: float32 [512], replicated, may hold values from 0.0009765625 to 0.0029296875
- k_ref: float32 [4], replicated, may hold values from 0.5 to 4
- sensitivity: float32 [4, 6], replicated, may hold values from -0.1 to 0.1
- decay: float32 [4], replicated, may hold values from 0.1 to 0.5
- material: int32 [512], P('space'), may hold values from 0 to 3
- neighbors: int32 [512, 4], P('space'), may hold values from -1 to 79, as said below
- send_list: int32 [8, 8, 2], P('space'), may hold values from 0 to 63, as said below
Outputs:
- residual: float32 [84, 32768], P(None, ('space', 'chaos'))
- jvp_out: float32 [84, 32768], P(None, ('space', 'chaos'))
Inputs may be any that keep to these rules, and one draw needn't show every extreme that they name: `neighbors`: -1 marks a face without neighbour. An entry below 64 is a block of the same partition; an entry 64 + t * 2 + j names slot j of what partition t sends here, where t is one or two indices away along space, cyclically, and the slot is live. send_list[s, t, j] is a local block of partition s. Only slots named by some neighbour entry are live: from s to a partition one or two indices away, cyclically, between 1 and 2 leading slots; to any other partition none.
All inputs are finite; a program needn't handle non-finite values.
Results may differ from a plain program's by a relative error of at most 0.0003.
Values sent between devices are 32-bit elements; how exact they have to be, the bound alone decides.
A program may use at most 192 MiB of HBM per device.

v0:
```python
import functools
import math

import jax
import jax.numpy as jnp
import numpy as np
from jax import lax
from jax.experimental import pallas as pl
from jax.experimental.pallas import tpu as pltpu
from jax.sharding import PartitionSpec as P

NMAT = 4
SITES = 64
TERMS = 84
MAIN = 80
LOG2E = 1.0 / math.log(2.0)
LN2 = math.log(2.0)
OFFSETS = (1, -1, 2, -2)
BF = jnp.bfloat16
F32 = jnp.float32


def compositions(remaining, places):
    if places == 1:
        return [[remaining]]
    listing = []
    for leading in range(remaining, -1, -1):
        for trailing in compositions(remaining - leading, places - 1):
            listing.append([leading] + trailing)
    return listing


def chaos_orders(variables):
    listing = []
    for degree in range(4):
        listing = listing + compositions(degree, variables)
    return np.array(listing, dtype=np.int32)


def products(nodes, orders, along):
    value = None
    for d in range(nodes.shape[1]):
        x = jnp.expand_dims(nodes[:, d], 1 - along)
        o = jnp.expand_dims(jnp.asarray(orders[:, d]), along)
        second = (x * x - 1.0) * np.float32(1.0 / math.sqrt(2.0))
        third = (x * x * x - 3.0 * x) * np.float32(1.0 / math.sqrt(6.0))
        factor = jnp.where(o == 0, 1.0, jnp.where(o == 1, x, jnp.where(o == 2, second, third)))
        value = factor if value is None else value * factor
    return value


def halves(x):
    high = lax.reduce_precision(x, 8, 7)
    return high, x - high


def tables(nodes, weights):
    orders = chaos_orders(nodes.shape[1])
    rest = np.arange(MAIN, TERMS)
    first = np.arange(MAIN)
    column = np.concatenate([first, first, first, rest, rest, rest, np.zeros(4, np.int64)])
    low = np.concatenate([np.zeros(160), np.ones(80), np.zeros(8), np.ones(4), np.zeros(4)])
    keep = np.concatenate([np.ones(252), np.zeros(4)])
    high, lower = halves(products(nodes, orders[column], 0))
    left = jnp.where(jnp.asarray(low[None, :] > 0), lower, high)
    left = jnp.where(jnp.asarray(keep[None, :] > 0), left, 0.0).astype(BF)
    back = np.concatenate([np.arange(TERMS), np.zeros(4, np.int64)])
    weighted = products(nodes, orders[back], 1) * weights[None, :]
    weighted = jnp.where(jnp.asarray(np.arange(88)[:, None] < TERMS), weighted, 0.0)
    high, lower = halves(weighted)
    right = jnp.concatenate([high, lower], 0).astype(BF)
    mass = jnp.sum(weighted, axis=1, keepdims=True)
    return left, right, mass


def place_rhs(rhs, face, field, main, tail):
    cols = slice(field * 128, field * 128 + 128)
    row = lax.broadcasted_iota(jnp.int32, (8, 128), 0)
    high = main.astype(BF)
    low = (main - high.astype(F32)).astype(BF)
    tail_high = tail.astype(BF).astype(F32)
    rhs[face, 0:80, cols] = high
    rhs[face, 80:160, cols] = low
    rhs[face, 160:240, cols] = high
    rhs[face, 240:256, cols] = jnp.concatenate(
        [
            jnp.where(row < 4, tail_high, tail - tail_high),
            jnp.where(row < 4, tail_high, 0.0),
        ],
        0,
    ).astype(BF)


def fields(x):
    row = lax.broadcasted_iota(jnp.int32, (8, 128), 0)
    mixed = x[160:168]
    turned = pltpu.roll(mixed, 4, 0)
    mode = (x[0:80], jnp.where(row < 4, mixed, turned))
    step = (x[80:160], jnp.where(row < 4, turned, mixed))
    aux = x[168:176]
    damp = aux[7:8]
    offset = jnp.where(row < 7, aux, 0.0)
    arg_main = mode[0] * damp
    arg_main = jnp.concatenate([arg_main[0:8] + offset, arg_main[8:80]], 0)
    arg = (arg_main, mode[1] * damp)
    rate = damp * LN2
    change = (step[0] * rate, step[1] * rate)
    return mode, step, arg, change


def pair_work(pair, base, ids, coefs, field, left, right, mass, source, res, jvp, rhs, kc, acc, own):
    lane = lax.broadcasted_iota(jnp.int32, (1, 128), 1)
    low_half = lane < 64
    height = lane % 64
    x = field[base + pair]
    mine = fields(x)
    place_rhs(rhs, 6, 0, *mine[2])
    place_rhs(rhs, 6, 1, *mine[3])
    for face in range(6):
        if face == 0:
            scale = jnp.where(height == 63, 0.0, 0.5)
            other = [tuple(pltpu.roll(a, 127, 1) for a in f) for f in mine]
            gap = [tuple((a - b) * scale for a, b in zip(mine[i], other[i])) for i in (0, 1)]
        elif face == 1:
            scale = jnp.where(height == 0, 1.0, 0.5)
            bottom = height == 0
            other = [tuple(pltpu.roll(a, 1, 1) for a in f) for f in mine]
            gap = [
                tuple((a - jnp.where(bottom, 0.0, b)) * scale for a, b in zip(mine[i], other[i]))
                for i in (0, 1)
            ]
            other = [
                tuple(jnp.where(bottom, a, b) for a, b in zip(mine[i], other[i])) for i in range(4)
            ]
        else:
            at = pair * 8 + (face - 2)
            e0 = ids[at]
            e1 = ids[at + 4]
            x0 = field[e0 // 2]
            x1 = field[e1 // 2]
            x0 = pltpu.roll(x0, (e0 % 2) * 64, 1)
            x1 = pltpu.roll(x1, (1 - e1 % 2) * 64, 1)
            scale = jnp.where(low_half, coefs[at], coefs[at + 4])
            other = fields(jnp.where(low_half, x0, x1))
            gap = [tuple((a - b) * scale for a, b in zip(mine[i], other[i])) for i in (0, 1)]
        place_rhs(rhs, face, 0, *gap[0])
        place_rhs(rhs, face, 1, *gap[1])
        place_rhs(rhs, face, 2, *other[2])
        place_rhs(rhs, face, 3, *other[3])
    total = None
    count = left.shape[0] // 512
    for part in range(count):
        rows = slice(part * 512, part * 512 + 512)
        basis = left[rows]
        r = jnp.dot(basis, rhs[6, :, 0:256], preferred_element_type=F32)
        conduct = jnp.exp2(r[:, 0:128])
        kc[0] = conduct
        kc[1] = conduct * r[:, 128:256]
        for face in range(6):
            r = jnp.dot(basis, rhs[face], preferred_element_type=F32)
            k = jnp.exp2(r[:, 256:384])
            a = kc[0] + k
            b = kc[1] + k * r[:, 384:512]
            gap = r[:, 0:128]
            bal = a * gap
            step = b * gap + a * r[:, 128:256]
            if face == 0:
                acc[0] = bal
                acc[1] = step
            else:
                acc[0] += bal
                acc[1] += step
        both = jnp.concatenate([acc[0], acc[1]], 1)
        high = both.astype(BF)
        low = (both - high.astype(F32)).astype(BF)
        w = right[:, rows]
        one = jnp.dot(w, high, preferred_element_type=F32)
        two = jnp.dot(w[0:88], low, preferred_element_type=F32)
        one = one[0:88] + one[88:176] + two
        total = one if total is None else total + one
    cols = pl.ds(pl.multiple_of(pair * 128, 128), 128)
    res[:, cols] = (total[:, 0:128] - mass[...] * source[:, cols])[0:TERMS]
    jvp[:, cols] = total[0:TERMS, 128:256]


def kernel(pairs, ids, coefs, start, field, left, right, mass, source, res, jvp, rhs, kc, acc):
    base = start[0]

    def body(pair, carry):
        pair_work(pair, base, ids, coefs, field, left, right, mass, source, res, jvp, rhs, kc, acc, None)
        return carry

    lax.fori_loop(0, pairs, body, 0)


def aux_rows(k_ref, sensitivity, decay, material):
    table = jnp.concatenate(
        [jnp.log(k_ref)[:, None], sensitivity, -decay[:, None]], axis=1
    ) * np.float32(LOG2E)
    mine = material.reshape(-1, 2)
    spread = jnp.repeat(mine, SITES, axis=1)[:, None, :]
    out = jnp.zeros((mine.shape[0], 8, 128), F32)
    for m in range(NMAT):
        out = jnp.where(spread == m, table[m][None, :, None], out)
    return out


def slots(neighbors, space_rank, space_count, chaos_rank, own_blocks, halo_depth):
    blocks = neighbors.shape[0]
    mine = lax.dynamic_slice_in_dim(neighbors, chaos_rank * own_blocks, own_blocks, 0)
    halo_ref = mine - blocks
    distance = (space_rank - halo_ref // halo_depth) % space_count
    order = jnp.where(
        distance == 1, 0, jnp.where(distance == space_count - 1, 1, jnp.where(distance == 2, 2, 3))
    )
    ids = jnp.where(mine >= blocks, blocks + order * halo_depth + halo_ref % halo_depth, mine)
    ids = jnp.maximum(ids, 0).reshape(-1)
    coefs = jnp.where(mine >= 0, 0.25, 0.0).astype(F32).reshape(-1)
    return ids, coefs


def per_device(
    chaos_modes, newton_heading, source, nodes, weights, k_ref, sensitivity, decay,
    material, neighbors, send_list,
):
    space_count = lax.axis_size("space")
    space_rank = lax.axis_index("space")
    chaos_rank = lax.axis_index("chaos")
    cells = chaos_modes.shape[1]
    pairs = cells // 128
    halo_depth = send_list.shape[2]
    packed = jnp.concatenate(
        [chaos_modes[:MAIN], newton_heading[:MAIN], chaos_modes[MAIN:], newton_heading[MAIN:]], 0
    )
    packed = packed.reshape(2 * TERMS, pairs, 128).transpose(1, 0, 2)
    everyone = lax.all_gather(packed, "chaos", axis=0, tiled=True)
    aux = aux_rows(k_ref, sensitivity, decay, material)
    local = jnp.concatenate([everyone, aux], axis=1)
    pieces = [local]
    for offset in OFFSETS:
        target = (space_rank + offset) % space_count
        rows = lax.dynamic_index_in_dim(send_list[0], target, 0, keepdims=False)
        picked = [
            lax.dynamic_slice(local, (rows[j] // 2, 0, (rows[j] % 2) * 64), (1, 176, 64))
            for j in range(halo_depth)
        ]
        outgoing = jnp.concatenate(picked, axis=2)
        pieces.append(
            lax.ppermute(
                outgoing, "space", [(i, (i + offset) % space_count) for i in range(space_count)]
            )
        )
    field = jnp.concatenate(pieces, axis=0)
    ids, coefs = slots(
        neighbors, space_rank, space_count, chaos_rank, cells // SITES, halo_depth
    )
    left, right, mass = tables(nodes, weights)
    start = (chaos_rank * pairs).astype(jnp.int32).reshape(1)
    vmem = pl.BlockSpec(memory_space=pltpu.VMEM)
    smem = pl.BlockSpec(memory_space=pltpu.SMEM)
    return pl.pallas_call(
        functools.partial(kernel, pairs),
        out_shape=[jax.ShapeDtypeStruct((TERMS, cells), F32)] * 2,
        in_specs=[smem, smem, smem, vmem, vmem, vmem, vmem, vmem],
        out_specs=[vmem, vmem],
        scratch_shapes=[
            pltpu.VMEM((7, 256, 512), BF),
            pltpu.VMEM((2, 512, 128), F32),
            pltpu.VMEM((2, 512, 128), F32),
        ],
        compiler_params=pltpu.CompilerParams(vmem_limit_bytes=48 * 1024 * 1024),
    )(ids, coefs, start, field, left, right, mass, source[None, :])


def solution(mesh):
    return jax.shard_map(
        per_device,
        mesh=mesh,
        in_specs=(
            P(None, ("space", "chaos")),
            P(None, ("space", "chaos")),
            P(("space", "chaos")),
            P(), P(), P(), P(), P(),
            P("space"),
            P("space", None),
            P("space", None, None),
        ),
        out_specs=(P(None, ("space", "chaos")), P(None, ("space", "chaos"))),
        check_vma=False,
    )
```

profile of v0, /device:TPU:0, one launch (start us, length us, event | category | flops | bytes accessed | tf_op | source)
XLA Modules:
  0.0 91.3 jit_solution(8743288119265190873)
XLA Ops:
  7.2 0.0 all-gather.2.cloned.1.call-start
  7.2 1.0 %slice.88 = f32[80,1024]{1,0:T(8,128)S(1)} slice(f32[84,1024]{1,0:T(8,128)} %param.26), slice={[0:80], [0:1024]} | slice | bytes 655360 | tf_op jit(solution)/shard_map/slice | solution.py:233
  8.2 0.8 slice.90
  9.0 1.0 %slice.89 = f32[80,1024]{1,0:T(8,128)S(1)} slice(f32[84,1024]{1,0:T(8,128)} %param.27), slice={[0:80], [0:1024]} | slice | bytes 655360 | tf_op jit(solution)/shard_map/slice | solution.py:233
  10.0 0.0 copy-start.27
  10.0 0.0 copy-start.28
  10.1 0.0 copy-start.30
  10.1 0.0 copy-start.31
  10.1 0.0 copy-start.32
  10.1 0.0 copy-start.33
  10.1 0.0 copy-start.34
  10.1 0.0 copy-start.35
  10.1 0.0 copy-start.37
  10.2 0.8 slice.91
  11.0 0.1 maximum_bitcast_fusion
  11.3 0.1 copy.45
  11.5 1.0 %copy.41 = f32[8,168,128]{2,1,0:T(8,128)} copy(f32[8,168,128]{2,0,1:T(8,128)S(1)} %bitcast.47) | data formatting | bytes 1376256 | tf_op jit(solution)/shard_map/transpose | solution.py:235
  12.4 0.0 all-gather.2.cloned.1.call-update
  12.6 0.1 constant_dynamic-slice_fusion
  12.6 0.6 fusion.55
  18.2 0.6 fusion.57
  34.1 0.7 broadcast_compare_fusion.3
  34.8 0.1 eq.248
  34.9 0.1 broadcast_in_dim.597
  35.0 0.1 eq.249
  35.1 0.1 eq.252
  35.2 0.1 broadcast_in_dim.602
  35.3 0.1 eq.253
  35.4 0.1 eq.256
  35.5 0.1 broadcast_in_dim.606
  35.6 0.1 eq.257
  35.7 0.1 eq.260
  35.8 0.1 broadcast_in_dim.610
  36.0 0.1 eq.261
  36.0 0.7 log_bitcast_fusion
  36.7 0.1 copy.42
  36.8 0.7 negate_bitcast_fusion
  37.5 0.1 copy.43
  37.8 1.2 %fusion.53 = (f32[88]{0:T(128)S(1)}, f32[88,512]{1,0:T(8,128)S(1)}) fusion(f32[512]{0:T(512)S(1)} %copy-done.5, f32[512]{0:T(512)S(1)} %get-tuple-element.72, f32[512]{0:T(512)S(1)} %get-tuple-element.73, pred[88]{0:T(512)(128)(4,1)} %constant.317, f32[512]{0:T(512)S(1)} %bitcast.61, pred[88]{0:T(512)(128)(4,1)} %constant.316, pred[88]{0:T(512)(128)(4,1)} %constant.315, ...), kind=kLoop, calls=%fused_computation.136 | loop fusion | flops 1171368 | bytes 221160 | tf_op jit(solution)/shard_map/reduce_sum | solution.py:72
  39.0 0.1 copy.44.mass
  39.1 0.1 fusion.45
  39.2 0.1 copy.39
  39.3 0.1 reshape.361.ids
  39.4 0.1 compare_select_fusion.1
  39.5 0.1 copy.40
  39.6 0.1 reshape.362.coefs
  39.7 0.1 maximum_multiply_fusion
  39.9 0.1 select_select_fusion
  40.2 1.5 %fusion.2.left = bf16[512,256]{1,0:T(8,128)(2,1)S(1)} fusion(f32[512]{0:T(512)S(1)} %bitcast.77, f32[512]{0:T(512)S(1)} %bitcast.76, f32[512]{0:T(512)S(1)} %bitcast.62, f32[512]{0:T(512)S(1)} %bitcast.75, f32[512]{0:T(512)S(1)} %bitcast.74, f32[512]{0:T(512)S(1)} %bitcast.65, f32[512]{0:T(512)S(1)} %bitcast.73, f32[512]{0:T(512)S(1)} %bitcast.72, ...), kind=kLoop, calls=%fused_computation.21 | loop fusion | flops 3670016 | bytes 304128 | tf_op jit(solution)/shard_map/convert_element_type | solution.py:66
  41.7 14.4 %all-gather.2.cloned.1.call-done = f32[32,168,128]{2,1,0:T(8,128)} async-done(((f32[8,168,128]{2,1,0:T(8,128)}), f32[32,168,128]{2,1,0:T(8,128)}) %all-gather.2.cloned.1.call-update) | async-done | bytes 2752528 | tf_op jit(solution)/shard_map/all_gather | solution.py:236
  56.1 1.3 %fusion.11 = (f32[1,176,64]{2,1,0:T(8,128)S(1)}, f32[1,176,64]{2,1,0:T(8,128)S(1)}, f32[1,176,64]{2,1,0:T(8,128)S(1)}, f32[1,176,64]{2,1,0:T(8,128)S(1)}) fusion(s32[]{:T(128)S(6)} %select_n.362, s32[]{:T(128)S(6)} %select_n.364, f32[32,168,128]{2,1,0:T(8,128)} %all-gather.2.cloned.1.call-done, f32[32,8,128]{2,1,0:T(8,128)S(1)} %select_select_fusion, ...), kind=kLoop, calls=%fused_computation.35 | loop fusion | flops 45056 | bytes 3063840 | tf_op jit(solution)/shard_map/concatenate | solution.py:238
  57.4 0.6 copy-done.1
  58.0 0.2 fusion.10
  58.2 0.1 pad_maximum_fusion.5
  58.3 3.4 %collective-permute-start.3 = (f32[1,176,128]{2,1,0:T(8,128)S(1)}, f32[1,176,128]{2,1,0:T(8,128)S(1)}, u32[]{:S(2)}, u32[]{:S(2)}) collective-permute-start(f32[1,176,128]{2,1,0:T(8,128)S(1)} %pad_maximum_fusion.5), channel_id=1, source_target_pairs={{0,24},{4,28},{8,0},{12,4},{16,8},{20,12},{24,16},{28,20},{1,25},{... | collective-permute-start | bytes 270344 | tf_op jit(solution)/shard_map/ppermute | solution.py:249
  61.7 0.1 pad_maximum_fusion.4
  61.8 0.1 collective-permute-start.2
  61.8 0.1 pad_maximum_fusion.3
  61.9 2.7 %collective-permute-start.1 = (f32[1,176,128]{2,1,0:T(8,128)S(1)}, f32[1,176,128]{2,1,0:T(8,128)S(1)}, u32[]{:S(2)}, u32[]{:S(2)}) collective-permute-start(f32[1,176,128]{2,1,0:T(8,128)S(1)} %pad_maximum_fusion.3), channel_id=1, source_target_pairs={{0,28},{4,0},{8,4},{12,8},{16,12},{20,16},{24,20},{28,24},{1,29},{... | collective-permute-start | bytes 270344 | tf_op jit(solution)/shard_map/ppermute | solution.py:249
  64.7 0.1 pad_maximum_fusion.2
  64.8 0.1 collective-permute-start
  64.8 0.2 fusion
  65.0 5.5 %collective-permute-done = f32[1,176,128]{2,1,0:T(8,128)S(1)} collective-permute-done((f32[1,176,128]{2,1,0:T(8,128)S(1)}, f32[1,176,128]{2,1,0:T(8,128)S(1)}, u32[]{:S(2)}, u32[]{:S(2)}) %collective-permute-start) | collective-permute-done | bytes 90144 | tf_op jit(solution)/shard_map/ppermute | solution.py:249
  70.7 13.7 %shard_map.257 = (f32[84,1024]{1,0:T(8,128)}, f32[84,1024]{1,0:T(8,128)}) custom-call(s32[64]{0:T(128)S(1)} %reshape.361.ids, f32[64]{0:T(128)S(1)} %reshape.362.coefs, s32[1]{0:T(128)} %bitcast.start, f32[36,176,128]{2,1,0:T(8,128)S(1)} %constant_dynamic-update-slice_fusion.field, bf16[512,256]{1,0:T(8,128)(2,1)S(1)} %fusion.2.left, ...), custom_call_target="tpu_custom_call" | custom-call | tf_op jit(solution)/shard_map/pallas_call | solution.py:261
  (88 shorter events, 0.4 us)
Async XLA Ops:
  7.2 48.9 %all-gather.2.cloned.1.call-start = ((), (), s32[]{:S(2)}) async-start(), calls=%async_computation | async-start | bytes 3440640 | tf_op jit(solution)/shard_map/all_gather | solution.py:236
  8.2 4.3 %copy-start.2 = (s32[1,8,2]{1,2,0:T(2,128)S(1)}, s32[1,8,2]{1,2,0:T(2,128)}, u32[]{:S(2)}) copy-start(s32[1,8,2]{1,2,0:T(2,128)} %param.36) | copy-start | bytes 196
  10.0 27.6 %copy-start.3 = (f32[512,6]{0,1:T(8,128)S(1)}, f32[512,6]{0,1:T(8,128)}, u32[]{:S(2)}) copy-start(f32[512,6]{0,1:T(8,128)} %param.29) | copy-start | bytes 36868
  10.0 27.7 %copy-start.5 = (f32[512]{0:T(512)S(1)}, f32[512]{0:T(512)}, u32[]{:S(2)}) copy-start(f32[512]{0:T(512)} %param.30) | copy-start | bytes 6148
  10.0 27.6 %copy-start.27 = (pred[88]{0:T(512)(128)(4,1)S(1)}, pred[88]{0:T(512)(128)(4,1)}, u32[]{:S(2)}) copy-start(pred[88]{0:T(512)(128)(4,1)} %constant.299) | copy-start | bytes 268
  10.0 27.6 %copy-start.28 = (pred[88]{0:T(512)(128)(4,1)S(1)}, pred[88]{0:T(512)(128)(4,1)}, u32[]{:S(2)}) copy-start(pred[88]{0:T(512)(128)(4,1)} %constant.300) | copy-start | bytes 268
  10.0 27.6 %copy-start.29 = (pred[88]{0:T(512)(128)(4,1)S(1)}, pred[88]{0:T(512)(128)(4,1)}, u32[]{:S(2)}) copy-start(pred[88]{0:T(512)(128)(4,1)} %constant.301) | copy-start | bytes 268
  10.1 27.6 %copy-start.30 = (pred[88]{0:T(512)(128)(4,1)S(1)}, pred[88]{0:T(512)(128)(4,1)}, u32[]{:S(2)}) copy-start(pred[88]{0:T(512)(128)(4,1)} %constant.302) | copy-start | bytes 268
  10.1 27.6 %copy-start.31 = (pred[88]{0:T(512)(128)(4,1)S(1)}, pred[88]{0:T(512)(128)(4,1)}, u32[]{:S(2)}) copy-start(pred[88]{0:T(512)(128)(4,1)} %constant.303) | copy-start | bytes 268
  10.1 27.6 %copy-start.32 = (pred[88]{0:T(512)(128)(4,1)S(1)}, pred[88]{0:T(512)(128)(4,1)}, u32[]{:S(2)}) copy-start(pred[88]{0:T(512)(128)(4,1)} %constant.304) | copy-start | bytes 268
  10.1 27.6 %copy-start.33 = (pred[88]{0:T(512)(128)(4,1)S(1)}, pred[88]{0:T(512)(128)(4,1)}, u32[]{:S(2)}) copy-start(pred[88]{0:T(512)(128)(4,1)} %constant.305) | copy-start | bytes 268
  10.1 27.6 %copy-start.34 = (pred[88]{0:T(512)(128)(4,1)S(1)}, pred[88]{0:T(512)(128)(4,1)}, u32[]{:S(2)}) copy-start(pred[88]{0:T(512)(128)(4,1)} %constant.306) | copy-start | bytes 268
  10.1 27.6 %copy-start.35 = (pred[88]{0:T(512)(128)(4,1)S(1)}, pred[88]{0:T(512)(128)(4,1)}, u32[]{:S(2)}) copy-start(pred[88]{0:T(512)(128)(4,1)} %constant.307) | copy-start | bytes 268
  10.1 27.6 %copy-start.36 = (pred[88]{0:T(512)(128)(4,1)S(1)}, pred[88]{0:T(512)(128)(4,1)}, u32[]{:S(2)}) copy-start(pred[88]{0:T(512)(128)(4,1)} %constant.308) | copy-start | bytes 268
  10.1 27.6 %copy-start.37 = (pred[88]{0:T(512)(128)(4,1)S(1)}, pred[88]{0:T(512)(128)(4,1)}, u32[]{:S(2)}) copy-start(pred[88]{0:T(512)(128)(4,1)} %constant.309) | copy-start | bytes 268
  10.2 27.6 %copy-start.38 = (pred[88]{0:T(512)(128)(4,1)S(1)}, pred[88]{0:T(512)(128)(4,1)}, u32[]{:S(2)}) copy-start(pred[88]{0:T(512)(128)(4,1)} %constant.310) | copy-start | bytes 268
  10.2 27.6 %copy-start.39 = (pred[88]{0:T(512)(128)(4,1)S(1)}, pred[88]{0:T(512)(128)(4,1)}, u32[]{:S(2)}) copy-start(pred[88]{0:T(512)(128)(4,1)} %constant.311) | copy-start | bytes 268
  10.2 27.6 %copy-start.40 = (pred[88]{0:T(512)(128)(4,1)S(1)}, pred[88]{0:T(512)(128)(4,1)}, u32[]{:S(2)}) copy-start(pred[88]{0:T(512)(128)(4,1)} %constant.312) | copy-start | bytes 268
  10.2 27.6 %copy-start.41 = (pred[88]{0:T(512)(128)(4,1)S(1)}, pred[88]{0:T(512)(128)(4,1)}, u32[]{:S(2)}) copy-start(pred[88]{0:T(512)(128)(4,1)} %constant.313) | copy-start | bytes 268
  11.0 28.1 %copy-start.4 = (s32[64,4]{0,1:T(4,128)S(1)}, s32[64,4]{0,1:T(4,128)}, u32[]{:S(2)}) copy-start(s32[64,4]{0,1:T(4,128)} %param.35) | copy-start | bytes 3076
  11.0 28.7 %copy-start.6 = (f32[4,6]{1,0:T(4,128)S(1)}, f32[4,6]{1,0:T(4,128)}, u32[]{:S(2)}) copy-start(f32[4,6]{1,0:T(4,128)} %param.32) | copy-start | bytes 292
  11.1 28.9 %copy-start.7 = (pred[256]{0:T(512)(128)(4,1)S(1)}, pred[256]{0:T(512)(128)(4,1)}, u32[]{:S(2)}) copy-start(pred[256]{0:T(512)(128)(4,1)} %constant.279) | copy-start | bytes 772
  11.1 28.9 %copy-start.8 = (pred[256]{0:T(512)(128)(4,1)S(1)}, pred[256]{0:T(512)(128)(4,1)}, u32[]{:S(2)}) copy-start(pred[256]{0:T(512)(128)(4,1)} %constant.280) | copy-start | bytes 772
  11.1 28.9 %copy-start.9 = (pred[256]{0:T(512)(128)(4,1)S(1)}, pred[256]{0:T(512)(128)(4,1)}, u32[]{:S(2)}) copy-start(pred[256]{0:T(512)(128)(4,1)} %constant.281) | copy-start | bytes 772
  11.1 28.9 %copy-start.10 = (pred[256]{0:T(512)(128)(4,1)S(1)}, pred[256]{0:T(512)(128)(4,1)}, u32[]{:S(2)}) copy-start(pred[256]{0:T(512)(128)(4,1)} %constant.282) | copy-start | bytes 772
  11.1 28.9 %copy-start.11 = (pred[256]{0:T(512)(128)(4,1)S(1)}, pred[256]{0:T(512)(128)(4,1)}, u32[]{:S(2)}) copy-start(pred[256]{0:T(512)(128)(4,1)} %constant.283) | copy-start | bytes 772
  11.2 28.9 %copy-start.12 = (pred[256]{0:T(512)(128)(4,1)S(1)}, pred[256]{0:T(512)(128)(4,1)}, u32[]{:S(2)}) copy-start(pred[256]{0:T(512)(128)(4,1)} %constant.284) | copy-start | bytes 772
  11.2 28.9 %copy-start.13 = (pred[256]{0:T(512)(128)(4,1)S(1)}, pred[256]{0:T(512)(128)(4,1)}, u32[]{:S(2)}) copy-start(pred[256]{0:T(512)(128)(4,1)} %constant.285) | copy-start | bytes 772
  11.2 28.9 %copy-start.14 = (pred[256]{0:T(512)(128)(4,1)S(1)}, pred[256]{0:T(512)(128)(4,1)}, u32[]{:S(2)}) copy-start(pred[256]{0:T(512)(128)(4,1)} %constant.286) | copy-start | bytes 772
  11.2 28.9 %copy-start.15 = (pred[256]{0:T(512)(128)(4,1)S(1)}, pred[256]{0:T(512)(128)(4,1)}, u32[]{:S(2)}) copy-start(pred[256]{0:T(512)(128)(4,1)} %constant.287) | copy-start | bytes 772
  11.2 28.9 %copy-start.16 = (pred[256]{0:T(512)(128)(4,1)S(1)}, pred[256]{0:T(512)(128)(4,1)}, u32[]{:S(2)}) copy-start(pred[256]{0:T(512)(128)(4,1)} %constant.288) | copy-start | bytes 772
  11.2 28.9 %copy-start.17 = (pred[256]{0:T(512)(128)(4,1)S(1)}, pred[256]{0:T(512)(128)(4,1)}, u32[]{:S(2)}) copy-start(pred[256]{0:T(512)(128)(4,1)} %constant.289) | copy-start | bytes 772
  11.2 28.9 %copy-start.18 = (pred[256]{0:T(512)(128)(4,1)S(1)}, pred[256]{0:T(512)(128)(4,1)}, u32[]{:S(2)}) copy-start(pred[256]{0:T(512)(128)(4,1)} %constant.290) | copy-start | bytes 772
  11.2 28.9 %copy-start.19 = (pred[256]{0:T(512)(128)(4,1)S(1)}, pred[256]{0:T(512)(128)(4,1)}, u32[]{:S(2)}) copy-start(pred[256]{0:T(512)(128)(4,1)} %constant.291) | copy-start | bytes 772
  11.3 28.9 %copy-start.20 = (pred[256]{0:T(512)(128)(4,1)S(1)}, pred[256]{0:T(512)(128)(4,1)}, u32[]{:S(2)}) copy-start(pred[256]{0:T(512)(128)(4,1)} %constant.292) | copy-start | bytes 772
  11.3 28.9 %copy-start.21 = (pred[256]{0:T(512)(128)(4,1)S(1)}, pred[256]{0:T(512)(128)(4,1)}, u32[]{:S(2)}) copy-start(pred[256]{0:T(512)(128)(4,1)} %constant.293) | copy-start | bytes 772
  11.3 28.9 %copy-start.22 = (pred[256]{0:T(512)(128)(4,1)S(1)}, pred[256]{0:T(512)(128)(4,1)}, u32[]{:S(2)}) copy-start(pred[256]{0:T(512)(128)(4,1)} %constant.294) | copy-start | bytes 772
  11.3 28.9 %copy-start.23 = (pred[256]{0:T(512)(128)(4,1)S(1)}, pred[256]{0:T(512)(128)(4,1)}, u32[]{:S(2)}) copy-start(pred[256]{0:T(512)(128)(4,1)} %constant.295) | copy-start | bytes 772
  11.3 28.9 %copy-start.24 = (pred[256]{0:T(512)(128)(4,1)S(1)}, pred[256]{0:T(512)(128)(4,1)}, u32[]{:S(2)}) copy-start(pred[256]{0:T(512)(128)(4,1)} %constant.296) | copy-start | bytes 772
  11.3 28.9 %copy-start.25 = (pred[256]{0:T(512)(128)(4,1)S(1)}, pred[256]{0:T(512)(128)(4,1)}, u32[]{:S(2)}) copy-start(pred[256]{0:T(512)(128)(4,1)} %constant.297) | copy-start | bytes 772
  11.3 28.9 %copy-start.26 = (pred[256]{0:T(512)(128)(4,1)S(1)}, pred[256]{0:T(512)(128)(4,1)}, u32[]{:S(2)}) copy-start(pred[256]{0:T(512)(128)(4,1)} %constant.298) | copy-start | bytes 772
  56.1 1.9 %copy-start.1 = (f32[32,168,128]{2,1,0:T(8,128)S(1)}, f32[32,168,128]{2,1,0:T(8,128)}, u32[]{:S(2)}) copy-start(f32[32,168,128]{2,1,0:T(8,128)} %all-gather.2.cloned.1.call-done) | copy-start | bytes 8257540
  58.3 12.4 %collective-permute-start.3 = (f32[1,176,128]{2,1,0:T(8,128)S(1)}, f32[1,176,128]{2,1,0:T(8,128)S(1)}, u32[]{:S(2)}, u32[]{:S(2)}) collective-permute-start(f32[1,176,128]{2,1,0:T(8,128)S(1)} %pad_maximum_fusion.5), channel_id=1, source_target_pairs={{0,24},{4,28},{8,0},{12,4},{16,8},{20,12},{24,16},{28,20},{1,25},{... | collective-permute-start | bytes 270344 | tf_op jit(solution)/shard_map/ppermute | solution.py:249
  61.8 8.9 %collective-permute-start.2 = (f32[1,176,128]{2,1,0:T(8,128)S(1)}, f32[1,176,128]{2,1,0:T(8,128)S(1)}, u32[]{:S(2)}, u32[]{:S(2)}) collective-permute-start(f32[1,176,128]{2,1,0:T(8,128)S(1)} %pad_maximum_fusion.4), channel_id=1, source_target_pairs={{0,8},{4,12},{8,16},{12,20},{16,24},{20,28},{24,0},{28,4},{1,9},{5... | collective-permute-start | bytes 270344 | tf_op jit(solution)/shard_map/ppermute | solution.py:249
  61.9 8.7 %collective-permute-start.1 = (f32[1,176,128]{2,1,0:T(8,128)S(1)}, f32[1,176,128]{2,1,0:T(8,128)S(1)}, u32[]{:S(2)}, u32[]{:S(2)}) collective-permute-start(f32[1,176,128]{2,1,0:T(8,128)S(1)} %pad_maximum_fusion.3), channel_id=1, source_target_pairs={{0,28},{4,0},{8,4},{12,8},{16,12},{20,16},{24,20},{28,24},{1,29},{... | collective-permute-start | bytes 270344 | tf_op jit(solution)/shard_map/ppermute | solution.py:249
  64.8 5.9 %copy-start = (f32[1024]{0:T(1024)S(1)}, f32[1024]{0:T(1024)}, u32[]{:S(2)}) copy-start(f32[1024]{0:T(1024)} %param.28) | copy-start | bytes 12292
  64.8 5.8 %collective-permute-start = (f32[1,176,128]{2,1,0:T(8,128)S(1)}, f32[1,176,128]{2,1,0:T(8,128)S(1)}, u32[]{:S(2)}, u32[]{:S(2)}) collective-permute-start(f32[1,176,128]{2,1,0:T(8,128)S(1)} %pad_maximum_fusion.2), channel_id=1, source_target_pairs={{0,4},{4,8},{8,12},{12,16},{16,20},{20,24},{24,28},{28,0},{1,5},{5... | collective-permute-start | bytes 270344 | tf_op jit(solution)/shard_map/ppermute | solution.py:249
Sparse Core Ops, SparseCore 0:
  12.6 43.4 all-gather.1
where the time goes:
time: 91.9 us; the launch traced here: 91.3 us
  between operations  35.4 us (39%)
  waiting for transfers between devices  19.9 us (22%)
  Pallas kernels  13.7 us (15%)
  local copies, waits for them, and re-layouts  9.42 us (10%)
  other arithmetic  6.54 us (7%)
  starting transfers between devices  6.28 us (7%)
    all_gather x1, waiting for transfers between devices, per_device(): everyone = lax.all_gather(packed, 'chaos', axis=0, tiled=True)  14.4 us
    pallas_call x1, Pallas kernels, per_device(): pl.pallas_call(functools.partial(kernel, pairs), out_shape=[jax.ShapeDtyp...  13.7 us
    ppermute x4, starting transfers between devices, per_device(): lax.ppermute(outgoing, 'space', [(i, (i + offset) % space_count) for i in...  6.24 us
    ppermute x4, waiting for transfers between devices, per_device(): lax.ppermute(outgoing, 'space', [(i, (i + offset) % space_count) for i in...  5.55 us
  transfers between devices with their start and end apart: 5, of which 2 were waited for; matrix products, arithmetic and copies ran while one was open for 10% of the time, Pallas kernels for 0%

commit v1 on v0

--- a/solution.py
+++ b/solution.py
@@ -37,40 +37,182 @@
     return np.array(listing, dtype=np.int32)
 
 
-def products(nodes, orders, along):
-    value = None
-    for d in range(nodes.shape[1]):
-        x = jnp.expand_dims(nodes[:, d], 1 - along)
-        o = jnp.expand_dims(jnp.asarray(orders[:, d]), along)
-        second = (x * x - 1.0) * np.float32(1.0 / math.sqrt(2.0))
-        third = (x * x * x - 3.0 * x) * np.float32(1.0 / math.sqrt(6.0))
-        factor = jnp.where(o == 0, 1.0, jnp.where(o == 1, x, jnp.where(o == 2, second, third)))
-        value = factor if value is None else value * factor
-    return value
-
-
-def halves(x):
-    high = lax.reduce_precision(x, 8, 7)
-    return high, x - high
-
-
-def tables(nodes, weights):
-    orders = chaos_orders(nodes.shape[1])
+def half_turn(x, wanted):
+    return jnp.where(wanted, pltpu.roll(x, 64, 1), x)
+
+
+def factors(x, o):
+    second = (x * x - 1.0) * np.float32(1.0 / math.sqrt(2.0))
+    third = (x * x * x - 3.0 * x) * np.float32(1.0 / math.sqrt(6.0))
+    return jnp.where(o == 0, 1.0, jnp.where(o == 1, x, jnp.where(o == 2, second, third)))
+
+
+def order_tables(dims):
+    orders = chaos_orders(dims)
     rest = np.arange(MAIN, TERMS)
     first = np.arange(MAIN)
     column = np.concatenate([first, first, first, rest, rest, rest, np.zeros(4, np.int64)])
-    low = np.concatenate([np.zeros(160), np.ones(80), np.zeros(8), np.ones(4), np.zeros(4)])
-    keep = np.concatenate([np.ones(252), np.zeros(4)])
-    high, lower = halves(products(nodes, orders[column], 0))
-    left = jnp.where(jnp.asarray(low[None, :] > 0), lower, high)
-    left = jnp.where(jnp.asarray(keep[None, :] > 0), left, 0.0).astype(BF)
     back = np.concatenate([np.arange(TERMS), np.zeros(4, np.int64)])
-    weighted = products(nodes, orders[back], 1) * weights[None, :]
-    weighted = jnp.where(jnp.asarray(np.arange(88)[:, None] < TERMS), weighted, 0.0)
-    high, lower = halves(weighted)
-    right = jnp.concatenate([high, lower], 0).astype(BF)
-    mass = jnp.sum(weighted, axis=1, keepdims=True)
-    return left, right, mass
+    return orders[column].T.copy(), orders[back].copy()
+
+
+def fill_tables(nodes, nodes_t, weights, order_left, order_right, left, right, mass):
+    dims = nodes.shape[1]
+    column = lax.broadcasted_iota(jnp.int32, (1, 256), 1)
+    lower = ((column >= 160) & (column < 240)) | ((column >= 248) & (column < 252))
+    step = 128
+
+    def body(part, carry):
+        rows = pl.ds(pl.multiple_of(part * step, step), step)
+        value = None
+        for d in range(dims):
+            f = factors(nodes[rows, d : d + 1], order_left[d : d + 1])
+            value = f if value is None else value * f
+        high = value.astype(BF).astype(F32)
+        value = jnp.where(lower, value - high, high)
+        left[rows] = jnp.where(column < 252, value, 0.0).astype(BF)
+        return carry
+
+    lax.fori_loop(0, nodes.shape[0] // step, body, 0)
+    row = lax.broadcasted_iota(jnp.int32, (88, 1), 0)
+    mass[...] = jnp.zeros(mass.shape, F32)
+
+    def body_right(part, carry):
+        cols = pl.ds(pl.multiple_of(part * step, step), step)
+        value = weights[:, cols]
+        for d in range(dims):
+            value = value * factors(nodes_t[d : d + 1, cols], order_right[:, d : d + 1])
+        value = jnp.where(row < TERMS, value, 0.0)
+        high = value.astype(BF).astype(F32)
+        right[:, cols] = jnp.concatenate([high, value - high], 0).astype(BF)
+        mass[...] += jnp.sum(value, axis=1, keepdims=True)
+        return carry
+
+    lax.fori_loop(0, nodes.shape[0] // step, body_right, 0)
+
+
+def remote(src, dst, send, recv, device):
+    return pltpu.make_async_remote_copy(
+        src_ref=src, dst_ref=dst, send_sem=send, recv_sem=recv,
+        device_id=device, device_id_type=pl.DeviceIdType.MESH,
+    )
+
+
+def pack_own(modes, heading, pairs, base, field):
+    for i in range(pairs):
+        cols = slice(i * 128, i * 128 + 128)
+        field[base + i, 0:80] = modes[0:80, cols]
+        field[base + i, 80:160] = heading[0:80, cols]
+        field[base + i, 160:168] = jnp.concatenate([modes[80:84, cols], heading[80:84, cols]], 0)
+
+
+def greet(space_count, chaos_count, space, chaos):
+    barrier = pltpu.get_barrier_semaphore()
+    if chaos_count == 4:
+        peers = [chaos + 1 - 2 * (chaos % 2), (chaos + 2) % 4]
+    else:
+        peers = [(chaos + k) % chaos_count for k in range(1, chaos_count)]
+    for peer in peers:
+        pl.semaphore_signal(
+            barrier, inc=1, device_id={"chaos": peer}, device_id_type=pl.DeviceIdType.MESH
+        )
+    for offset in OFFSETS:
+        pl.semaphore_signal(
+            barrier, inc=1, device_id={"space": (space + offset + space_count) % space_count},
+            device_id_type=pl.DeviceIdType.MESH,
+        )
+    pl.semaphore_wait(barrier, len(peers) + len(OFFSETS))
+    return peers
+
+
+def spread_modes(chaos_count, peers, chaos, pairs, field, send, recv, meanwhile):
+    def block(owner, first, count):
+        return field.at[pl.ds(owner * pairs + first, count), 0:168]
+
+    if chaos_count == 4:
+        across, along = peers
+        half = pairs // 2
+        plan = [
+            (chaos, 0, across), (chaos, half, along),
+            (chaos, half, across), (chaos, 0, along),
+        ]
+        copies = [
+            remote(block(o, f, half), block(o, f, half), send.at[i], recv.at[i], {"chaos": t})
+            for i, (o, f, t) in enumerate(plan)
+        ]
+        for copy in copies:
+            copy.start()
+        meanwhile()
+        copies[0].wait_recv()
+        on = remote(
+            block(across, 0, half), block(across, 0, half), send.at[4], recv.at[4],
+            {"chaos": along},
+        )
+        on.start()
+        copies[1].wait_recv()
+        over = remote(
+            block(along, half, half), block(along, half, half), send.at[5], recv.at[5],
+            {"chaos": across},
+        )
+        over.start()
+        copies[2].wait_recv()
+        copies[3].wait_recv()
+        on.wait_recv()
+        over.wait_recv()
+        return copies + [on, over]
+    copies = [
+        remote(
+            block(chaos, 0, pairs), block(chaos, 0, pairs), send.at[i], recv.at[i], {"chaos": t}
+        )
+        for i, t in enumerate(peers)
+    ]
+    for copy in copies:
+        copy.start()
+    meanwhile()
+    for copy in copies:
+        copy.wait_recv()
+    return copies
+
+
+def send_halo(space_count, space, picks, field, out, inbox, send, recv):
+    low_half = lax.broadcasted_iota(jnp.int32, (1, 128), 1) < 64
+    copies = []
+    for i, offset in enumerate(OFFSETS):
+        target = (space + offset + space_count) % space_count
+        e0 = picks[2 * target]
+        e1 = picks[2 * target + 1]
+        x0 = half_turn(field[e0 // 2], e0 % 2 == 1)
+        x1 = half_turn(field[e1 // 2], e1 % 2 == 0)
+        out[i] = jnp.where(low_half, x0, x1)
+        copy = remote(out.at[i], inbox.at[i], send.at[i], recv.at[i], {"space": target})
+        copy.start()
+        copies.append(copy)
+    return copies
+
+
+def gather_kernel(
+    sizes, picks, modes, heading, aux, nodes, nodes_t, weights, order_left, order_right,
+    field, left, right, mass, out, inbox, send, recv, halo_send, halo_recv,
+):
+    space_count, chaos_count, pairs = sizes
+    space = lax.axis_index("space")
+    chaos = lax.axis_index("chaos")
+    blocks = aux.shape[0] * 2
+    field[0 : blocks // 2, 168:176] = aux[...]
+    pack_own(modes, heading, pairs, chaos * pairs, field)
+    peers = greet(space_count, chaos_count, space, chaos)
+    copies = spread_modes(
+        chaos_count, peers, chaos, pairs, field, send, recv,
+        lambda: fill_tables(
+            nodes, nodes_t, weights, order_left, order_right, left, right, mass
+        ),
+    )
+    halo = send_halo(space_count, space, picks, field, out, inbox, halo_send, halo_recv)
+    for copy in copies:
+        copy.wait_send()
+    for i, copy in enumerate(halo):
+        copy.wait()
+        field[blocks // 2 + i] = inbox[i]
 
 
 def place_rhs(rhs, face, field, main, tail):
@@ -136,10 +278,8 @@
             at = pair * 8 + (face - 2)
             e0 = ids[at]
             e1 = ids[at + 4]
-            x0 = field[e0 // 2]
-            x1 = field[e1 // 2]
-            x0 = pltpu.roll(x0, (e0 % 2) * 64, 1)
-            x1 = pltpu.roll(x1, (1 - e1 % 2) * 64, 1)
+            x0 = half_turn(field[e0 // 2], e0 % 2 == 1)
+            x1 = half_turn(field[e1 // 2], e1 % 2 == 0)
             scale = jnp.where(low_half, coefs[at], coefs[at + 4])
             other = fields(jnp.where(low_half, x0, x1))
             gap = [tuple((a - b) * scale for a, b in zip(mine[i], other[i])) for i in (0, 1)]
@@ -229,35 +369,41 @@
     cells = chaos_modes.shape[1]
     pairs = cells // 128
     halo_depth = send_list.shape[2]
-    packed = jnp.concatenate(
-        [chaos_modes[:MAIN], newton_heading[:MAIN], chaos_modes[MAIN:], newton_heading[MAIN:]], 0
-    )
-    packed = packed.reshape(2 * TERMS, pairs, 128).transpose(1, 0, 2)
-    everyone = lax.all_gather(packed, "chaos", axis=0, tiled=True)
+    queue = nodes.shape[0]
+    blocks = material.shape[0]
     aux = aux_rows(k_ref, sensitivity, decay, material)
-    local = jnp.concatenate([everyone, aux], axis=1)
-    pieces = [local]
-    for offset in OFFSETS:
-        target = (space_rank + offset) % space_count
-        rows = lax.dynamic_index_in_dim(send_list[0], target, 0, keepdims=False)
-        picked = [
-            lax.dynamic_slice(local, (rows[j] // 2, 0, (rows[j] % 2) * 64), (1, 176, 64))
-            for j in range(halo_depth)
-        ]
-        outgoing = jnp.concatenate(picked, axis=2)
-        pieces.append(
-            lax.ppermute(
-                outgoing, "space", [(i, (i + offset) % space_count) for i in range(space_count)]
-            )
-        )
-    field = jnp.concatenate(pieces, axis=0)
+    order_left, order_right = order_tables(nodes.shape[1])
+    vmem = pl.BlockSpec(memory_space=pltpu.VMEM)
+    smem = pl.BlockSpec(memory_space=pltpu.SMEM)
+    field, left, right, mass = pl.pallas_call(
+        functools.partial(gather_kernel, (space_count, lax.axis_size("chaos"), pairs)),
+        out_shape=[
+            jax.ShapeDtypeStruct((blocks // 2 + 4, 176, 128), F32),
+            jax.ShapeDtypeStruct((queue, 256), BF),
+            jax.ShapeDtypeStruct((176, queue), BF),
+            jax.ShapeDtypeStruct((88, 1), F32),
+        ],
+        in_specs=[smem] + [vmem] * 8,
+        out_specs=[vmem] * 4,
+        scratch_shapes=[
+            pltpu.VMEM((4, 176, 128), F32),
+            pltpu.VMEM((4, 176, 128), F32),
+            pltpu.SemaphoreType.DMA((16,)),
+            pltpu.SemaphoreType.DMA((16,)),
+            pltpu.SemaphoreType.DMA((4,)),
+            pltpu.SemaphoreType.DMA((4,)),
+        ],
+        compiler_params=pltpu.CompilerParams(
+            collective_id=0, has_side_effects=True, vmem_limit_bytes=32 * 1024 * 1024
+        ),
+    )(
+        send_list.reshape(-1), chaos_modes, newton_heading, aux, nodes, nodes.T,
+        weights[None, :], jnp.asarray(order_left), jnp.asarray(order_right),
+    )
     ids, coefs = slots(
         neighbors, space_rank, space_count, chaos_rank, cells // SITES, halo_depth
     )
-    left, right, mass = tables(nodes, weights)
     start = (chaos_rank * pairs).astype(jnp.int32).reshape(1)
-    vmem = pl.BlockSpec(memory_space=pltpu.VMEM)
-    smem = pl.BlockSpec(memory_space=pltpu.SMEM)
     return pl.pallas_call(
         functools.partial(kernel, pairs),
         out_shape=[jax.ShapeDtypeStruct((TERMS, cells), F32)] * 2,

time: 91.9 us -> 64.8 us (0.71)
  Pallas kernels: 13.7 us -> 50.1 us
  between operations: 35.4 us -> 0.74 us
  waiting for transfers between devices: 19.9 us -> 0 us
  starting transfers between devices: 6.28 us -> 0 us
  other arithmetic: 6.54 us -> 3.73 us
    pallas_call x0 -> x1, Pallas kernels: none -> 36.9 us  [per_device(): pl.pallas_call(functools.partial(gather_kernel, (space_count, lax.axis_si...]
    all_gather x1 -> x0, waiting for transfers between devices: 14.4 us -> none  [per_device(): everyone = lax.all_gather(packed, 'chaos', axis=0, tiled=True)]
    ppermute x4 -> x0, starting transfers between devices: 6.24 us -> none  [per_device(): lax.ppermute(outgoing, 'space', [(i, (i + offset) % space_count) for i in...]
    unnamed x88 -> x16, local copies, waits for them, and re-layouts: 1.04 us -> 7.15 us
    ppermute x4 -> x0, waiting for transfers between devices: 5.55 us -> none  [per_device(): lax.ppermute(outgoing, 'space', [(i, (i + offset) % space_count) for i in...]
    slice x6 -> x0, local copies, waits for them, and re-layouts: 4.77 us -> none  [the longest x2 1.2 us: per_device(): rows[j] // 2]
    concatenate x7 -> x0, other arithmetic: 1.85 us -> none  [the longest x2 1.47 us: per_device(): local = jnp.concatenate([everyone, aux], axis=1)]
    convert_element_type x1 -> x0, other arithmetic: 1.48 us -> none  [tables(): left = jnp.where(jnp.asarray(keep[None, :] > 0), left, 0.0).astype(BF)]
  transfers between devices with their start and end apart: 5 -> 0, of which waited for: 2 -> 0; matrix products, arithmetic and copies ran while one was open for 10% -> 0% of each run, Pallas kernels for 0% -> 0%
where the time goes in v1:
time: 64.8 us; the launch traced here: 64.2 us
  Pallas kernels  50.1 us (77%)
  local copies, waits for them, and re-layouts  9.64 us (15%)
  other arithmetic  3.73 us (6%)
  between operations  0.74 us (1%)
    pallas_call x1, Pallas kernels, per_device(): pl.pallas_call(functools.partial(gather_kernel, (space_count, lax.axis_si...  36.9 us
    pallas_call x1, Pallas kernels, per_device(): pl.pallas_call(functools.partial(kernel, pairs), out_shape=[jax.ShapeDtyp...  13.2 us
    unnamed x16, local copies, waits for them, and re-layouts  7.15 us

profile of v1, /device:TPU:0, one launch (start us, length us, event | category | flops | bytes accessed | tf_op | source)
XLA Modules:
  0.0 64.2 jit_solution(13277436992988747507)
XLA Ops:
  0.6 0.7 %log_bitcast_fusion = f32[4,1]{0,1:T(1,128)S(1)} fusion(f32[4]{0:T(128)} %param.18), kind=kLoop, calls=%fused_computation.23 | loop fusion | bytes 32 | tf_op jit(solution)/shard_map/broadcast_in_dim | solution.py:338
  1.3 0.7 %negate_bitcast_fusion = f32[4,1]{0,1:T(1,128)S(1)} fusion(f32[4]{0:T(128)} %param.20), kind=kLoop, calls=%fused_computation.22 | loop fusion | flops 4 | bytes 32 | tf_op jit(solution)/shard_map/neg | solution.py:338
  2.0 0.1 copy.25
  2.1 0.1 copy.24
  2.1 0.8 %maximum_multiply_fusion = f32[4,8]{1,0:T(4,128)S(1)} fusion(f32[4,1]{1,0:T(4,128)S(1)} %copy.25, f32[4,6]{1,0:T(4,128)} %param.19, f32[4,1]{1,0:T(4,128)S(1)} %copy.24), kind=kLoop, calls=%fused_computation.14 | loop fusion | flops 96 | bytes 256 | tf_op jit(solution)/shard_map/mul | solution.py:337
  2.9 0.8 %fusion.3 = s32[16,4]{0,1:T(4,128)S(1)} fusion(s32[64,4]{0,1:T(4,128)} %param.22, s32[]{:T(128)S(6)} %select_n.50, s32[]{:T(128)S(6)} %axis_index.25), kind=kLoop, calls=%fused_computation.13 | loop fusion | flops 2816 | bytes 520 | tf_op jit(solution)/shard_map/max | solution.py:357
  3.7 0.8 %compare_select_fusion.1 = f32[16,4]{0,1:T(4,128)S(1)} fusion(s32[64,4]{0,1:T(4,128)} %param.22, s32[]{:T(128)S(6)} %select_n.50), kind=kLoop, calls=%fused_computation.17 | loop fusion | flops 128 | bytes 516 | tf_op jit(solution)/shard_map/jit(_where)/select_n | solution.py:358
  4.4 0.7 %broadcast_compare_fusion.3 = (pred[64]{0:T(512)(128)(4,1)S(1)}, pred[64]{0:T(512)(128)(4,1)S(1)}, pred[64]{0:T(512)(128)(4,1)S(1)}, pred[64]{0:T(512)(128)(4,1)S(1)}) fusion(s32[64]{0:T(128)} %param.21), kind=kLoop, calls=%fused_computation.27 | loop fusion | flops 256 | bytes 512 | tf_op jit(solution)/shard_map/eq | solution.py:344
  5.1 0.1 eq.91
  5.2 0.1 eq.95
  5.3 0.1 eq.103
  5.5 0.1 eq.99
  5.6 0.8 %copy.23 = s32[1,8,2]{2,1,0:T(8,128)S(1)} copy(s32[1,8,2]{1,2,0:T(2,128)} %param.23) | data formatting | bytes 128 | tf_op args[10]
  6.3 0.1 reshape.69.picks
  6.4 0.1 copy.22
  6.5 0.1 reshape.67.coefs
  6.6 0.1 copy.21
  6.7 0.1 reshape.66.ids
  6.8 0.1 broadcast_in_dim.105
  6.9 0.1 eq.100
  7.0 0.1 broadcast_in_dim.109
  7.1 0.1 eq.104
  7.2 0.1 broadcast_in_dim.101
  7.3 0.1 eq.96
  7.4 0.1 broadcast_in_dim.96
  7.5 0.1 eq.92
  7.6 0.1 select_select_fusion.aux
  7.7 0.9 %copy.26.nodes = f32[512,6]{1,0:T(8,128)S(1)} copy(f32[512,6]{0,1:T(8,128)} %param.16) | data formatting | bytes 24576 | tf_op args[3]
  8.6 0.0 copy-start
  8.6 1.0 %copy-done = f32[84,1024]{1,0:T(8,128)S(1)} copy-done((f32[84,1024]{1,0:T(8,128)S(1)}, f32[84,1024]{1,0:T(8,128)}, u32[]{:S(2)}) %copy-start) | copy-done | bytes 344088
  9.5 0.0 copy-start.1
  9.5 1.0 %copy-done.1 = f32[84,1024]{1,0:T(8,128)S(1)} copy-done((f32[84,1024]{1,0:T(8,128)S(1)}, f32[84,1024]{1,0:T(8,128)}, u32[]{:S(2)}) %copy-start.1) | copy-done | bytes 344088
  10.5 0.0 copy-start.2
  10.5 0.7 %copy-done.2 = f32[512,6]{0,1:T(8,128)S(1)} copy-done((f32[512,6]{0,1:T(8,128)S(1)}, f32[512,6]{0,1:T(8,128)}, u32[]{:S(2)}) %copy-start.2) | copy-done | bytes 12312
  11.2 0.0 copy-start.3
  11.2 0.8 %copy-done.3 = s32[88,6]{1,0:T(8,128)S(1)} copy-done((s32[88,6]{1,0:T(8,128)S(1)}, s32[88,6]{1,0:T(8,128)}, u32[]{:S(2)}) %copy-start.3) | copy-done | bytes 2136
  12.0 0.0 copy-start.4
  12.0 0.7 %copy-done.4 = s32[6,256]{1,0:T(8,128)S(1)} copy-done((s32[6,256]{1,0:T(8,128)S(1)}, s32[6,256]{1,0:T(8,128)}, u32[]{:S(2)}) %copy-start.4) | copy-done | bytes 6168
  12.7 0.0 copy-start.6
  12.7 0.7 %copy-done.6 = f32[512]{0:T(512)S(1)} copy-done((f32[512]{0:T(512)S(1)}, f32[512]{0:T(512)}, u32[]{:S(2)}) %copy-start.6) | copy-done | bytes 2072
  13.4 36.9 %shard_map.140 = (f32[36,176,128]{2,1,0:T(8,128)S(1)}, bf16[512,256]{1,0:T(8,128)(2,1)S(1)}, bf16[176,512]{1,0:T(8,128)(2,1)S(1)}, f32[88,1]{1,0:T(8,128)S(1)}) custom-call(s32[16]{0:T(128)S(1)} %reshape.69.picks, f32[84,1024]{1,0:T(8,128)S(1)} %copy-done, f32[84,1024]{1,0:T(8,128)S(1)} %copy-done.1, f32[32,8,128]{2,1,0:T(8,128)S(1)} %select_select_fusion.aux, ...), custom_call_target="tpu_custom_call" | custom-call | tf_op jit(solution)/shard_map/pallas_call | solution.py:378
  50.3 0.0 copy-start.5
  50.3 0.7 %copy-done.5 = f32[1024]{0:T(1024)S(1)} copy-done((f32[1024]{0:T(1024)S(1)}, f32[1024]{0:T(1024)}, u32[]{:S(2)}) %copy-start.5) | copy-done | bytes 4120
  51.0 13.2 %shard_map.141 = (f32[84,1024]{1,0:T(8,128)}, f32[84,1024]{1,0:T(8,128)}) custom-call(s32[64]{0:T(128)S(1)} %reshape.66.ids, f32[64]{0:T(128)S(1)} %reshape.67.coefs, s32[1]{0:T(128)} %bitcast.start, f32[36,176,128]{2,1,0:T(8,128)S(1)} %get-tuple-element.6.field, bf16[512,256]{1,0:T(8,128)(2,1)S(1)} %get-tuple-element.7.left, ...), custom_call_target="tpu_custom_call" | custom-call | tf_op jit(solution)/shard_map/pallas_call | solution.py:407
  (1 shorter events, 0.0 us)
Async XLA Ops:
  8.6 1.0 %copy-start = (f32[84,1024]{1,0:T(8,128)S(1)}, f32[84,1024]{1,0:T(8,128)}, u32[]{:S(2)}) copy-start(f32[84,1024]{1,0:T(8,128)} %modes.1) | copy-start | bytes 1032196
  9.5 1.0 %copy-start.1 = (f32[84,1024]{1,0:T(8,128)S(1)}, f32[84,1024]{1,0:T(8,128)}, u32[]{:S(2)}) copy-start(f32[84,1024]{1,0:T(8,128)} %heading.1) | copy-start | bytes 1032196
  10.5 0.7 %copy-start.2 = (f32[512,6]{0,1:T(8,128)S(1)}, f32[512,6]{0,1:T(8,128)}, u32[]{:S(2)}) copy-start(f32[512,6]{0,1:T(8,128)} %param.16) | copy-start | bytes 36868
  11.2 0.8 %copy-start.3 = (s32[88,6]{1,0:T(8,128)S(1)}, s32[88,6]{1,0:T(8,128)}, u32[]{:S(2)}) copy-start(s32[88,6]{1,0:T(8,128)} %constant.77.clone.order_right) | copy-start | bytes 6340
  12.0 0.7 %copy-start.4 = (s32[6,256]{1,0:T(8,128)S(1)}, s32[6,256]{1,0:T(8,128)}, u32[]{:S(2)}) copy-start(s32[6,256]{1,0:T(8,128)} %constant.76.clone.order_left) | copy-start | bytes 18436
  12.7 0.7 %copy-start.6 = (f32[512]{0:T(512)S(1)}, f32[512]{0:T(512)}, u32[]{:S(2)}) copy-start(f32[512]{0:T(512)} %param.17) | copy-start | bytes 6148
  50.3 0.7 %copy-start.5 = (f32[1024]{0:T(1024)S(1)}, f32[1024]{0:T(1024)}, u32[]{:S(2)}) copy-start(f32[1024]{0:T(1024)} %param.15) | copy-start | bytes 12292

commit v2 on v1

--- a/solution.py
+++ b/solution.py
@@ -47,48 +47,68 @@
     return jnp.where(o == 0, 1.0, jnp.where(o == 1, x, jnp.where(o == 2, second, third)))
 
 
-def order_tables(dims):
+def order_codes(dims):
     orders = chaos_orders(dims)
+    code = (orders * 4 ** np.arange(dims)[None, :]).sum(1)
     rest = np.arange(MAIN, TERMS)
     first = np.arange(MAIN)
     column = np.concatenate([first, first, first, rest, rest, rest, np.zeros(4, np.int64)])
-    back = np.concatenate([np.arange(TERMS), np.zeros(4, np.int64)])
-    return orders[column].T.copy(), orders[back].copy()
-
-
-def fill_tables(nodes, nodes_t, weights, order_left, order_right, left, right, mass):
-    dims = nodes.shape[1]
-    column = lax.broadcasted_iota(jnp.int32, (1, 256), 1)
-    lower = ((column >= 160) & (column < 240)) | ((column >= 248) & (column < 252))
-    step = 128
-
-    def body(part, carry):
-        rows = pl.ds(pl.multiple_of(part * step, step), step)
-        value = None
-        for d in range(dims):
-            f = factors(nodes[rows, d : d + 1], order_left[d : d + 1])
-            value = f if value is None else value * f
-        high = value.astype(BF).astype(F32)
-        value = jnp.where(lower, value - high, high)
-        left[rows] = jnp.where(column < 252, value, 0.0).astype(BF)
-        return carry
-
-    lax.fori_loop(0, nodes.shape[0] // step, body, 0)
+    out = np.zeros((8, 256), np.float32)
+    out[0] = code[column]
+    out[1, :TERMS] = code
+    return out
+
+
+def upright(row):
+    return jnp.transpose(jnp.broadcast_to(row, (128, 128)))
+
+
+def fill_tables(nodes_t, weights, codes, left, right, mass):
+    dims = nodes_t.shape[0]
+    column = lax.broadcasted_iota(jnp.int32, (1, 128), 1)
+    code_right = upright(codes[1:2, 0:128])[0:88].astype(jnp.int32)
     row = lax.broadcasted_iota(jnp.int32, (88, 1), 0)
     mass[...] = jnp.zeros(mass.shape, F32)
 
-    def body_right(part, carry):
-        cols = pl.ds(pl.multiple_of(part * step, step), step)
-        value = weights[:, cols]
+    def body(part, carry):
+        span = pl.ds(pl.multiple_of(part * 128, 128), 128)
+        points = [nodes_t[d : d + 1, span] for d in range(dims)]
+        stood = [upright(x) for x in points]
+        for side in range(2):
+            code = codes[0:1, side * 128 : side * 128 + 128].astype(jnp.int32)
+            at = column + side * 128
+            lower = ((at >= 160) & (at < 240)) | ((at >= 248) & (at < 252))
+            value = None
+            for d in range(dims):
+                f = factors(stood[d], (code // 4**d) % 4)
+                value = f if value is None else value * f
+            high = value.astype(BF).astype(F32)
+            value = jnp.where(lower, value - high, high)
+            left[span, side * 128 : side * 128 + 128] = jnp.where(at < 252, value, 0.0).astype(BF)
+        value = weights[:, span]
         for d in range(dims):
-            value = value * factors(nodes_t[d : d + 1, cols], order_right[:, d : d + 1])
+            value = value * factors(points[d], (code_right // 4**d) % 4)
         value = jnp.where(row < TERMS, value, 0.0)
         high = value.astype(BF).astype(F32)
-        right[:, cols] = jnp.concatenate([high, value - high], 0).astype(BF)
+        right[:, span] = jnp.concatenate([high, value - high], 0).astype(BF)
         mass[...] += jnp.sum(value, axis=1, keepdims=True)
         return carry
 
-    lax.fori_loop(0, nodes.shape[0] // step, body_right, 0)
+    lax.fori_loop(0, nodes_t.shape[1] // 128, body, 0)
+
+
+def fill_aux(k_ref, sensitivity, decay, material, table, field):
+    row = lax.broadcasted_iota(jnp.int32, (8, 128), 0)
+    low_half = lax.broadcasted_iota(jnp.int32, (8, 128), 1) < 64
+    dims = sensitivity.shape[1]
+    for m in range(NMAT):
+        tile = jnp.log(jnp.full((8, 128), k_ref[m], F32))
+        for d in range(dims):
+            tile = jnp.where(row == d + 1, sensitivity[m, d], tile)
+        tile = jnp.where(row == 7, -decay[m], tile)
+        table[m] = tile * np.float32(LOG2E)
+    for i in range(material.shape[0] // 2):
+        field[i, 168:176] = jnp.where(low_half, table[material[2 * i]], table[material[2 * i + 1]])
 
 
 def remote(src, dst, send, recv, device):
@@ -191,21 +211,34 @@
 
 
 def gather_kernel(
-    sizes, picks, modes, heading, aux, nodes, nodes_t, weights, order_left, order_right,
-    field, left, right, mass, out, inbox, send, recv, halo_send, halo_recv,
+    sizes, picks, k_ref, sensitivity, decay, material, modes_far, heading_far, nodes_far,
+    weights_far, codes_far, field, left, right, mass,
+    modes, heading, nodes_t, weights, codes, table, out, inbox,
+    send, recv, halo_send, halo_recv, near,
 ):
     space_count, chaos_count, pairs = sizes
     space = lax.axis_index("space")
     chaos = lax.axis_index("chaos")
-    blocks = aux.shape[0] * 2
-    field[0 : blocks // 2, 168:176] = aux[...]
+    blocks = material.shape[0]
+    loads = [
+        pltpu.make_async_copy(a, b, near.at[i])
+        for i, (a, b) in enumerate(
+            [
+                (modes_far, modes), (heading_far, heading), (nodes_far, nodes_t),
+                (weights_far, weights), (codes_far, codes),
+            ]
+        )
+    ]
+    for load in loads:
+        load.start()
+    fill_aux(k_ref, sensitivity, decay, material, table, field)
+    for load in loads:
+        load.wait()
     pack_own(modes, heading, pairs, chaos * pairs, field)
     peers = greet(space_count, chaos_count, space, chaos)
     copies = spread_modes(
         chaos_count, peers, chaos, pairs, field, send, recv,
-        lambda: fill_tables(
-            nodes, nodes_t, weights, order_left, order_right, left, right, mass
-        ),
+        lambda: fill_tables(nodes_t, weights, codes, left, right, mass),
     )
     halo = send_halo(space_count, space, picks, field, out, inbox, halo_send, halo_recv)
     for copy in copies:
@@ -250,7 +283,24 @@
     return mode, step, arg, change
 
 
-def pair_work(pair, base, ids, coefs, field, left, right, mass, source, res, jvp, rhs, kc, acc, own):
+def slot(neighbors, block, face, ranks, halo_depth):
+    space, space_count, blocks = ranks
+    entry = neighbors[block, face]
+    away = jnp.maximum(entry - blocks, 0)
+    distance = (space - away // halo_depth + space_count) % space_count
+    order = jnp.where(
+        distance == 1, 0, jnp.where(distance == space_count - 1, 1, jnp.where(distance == 2, 2, 3))
+    )
+    index = jnp.where(
+        entry >= blocks, blocks + order * halo_depth + away % halo_depth, jnp.maximum(entry, 0)
+    )
+    return index, jnp.where(entry >= 0, np.float32(0.25), np.float32(0.0))
+
+
+def pair_work(
+    pair, base, ranks, halo_depth, neighbors, field, left, right, mass, source, res, jvp, rhs,
+    kc, acc,
+):
     lane = lax.broadcasted_iota(jnp.int32, (1, 128), 1)
     low_half = lane < 64
     height = lane % 64
@@ -275,12 +325,11 @@
                 tuple(jnp.where(bottom, a, b) for a, b in zip(mine[i], other[i])) for i in range(4)
             ]
         else:
-            at = pair * 8 + (face - 2)
-            e0 = ids[at]
-            e1 = ids[at + 4]
+            e0, c0 = slot(neighbors, 2 * (base + pair), face - 2, ranks, halo_depth)
+            e1, c1 = slot(neighbors, 2 * (base + pair) + 1, face - 2, ranks, halo_depth)
             x0 = half_turn(field[e0 // 2], e0 % 2 == 1)
             x1 = half_turn(field[e1 // 2], e1 % 2 == 0)
-            scale = jnp.where(low_half, coefs[at], coefs[at + 4])
+            scale = jnp.where(low_half, c0, c1)
             other = fields(jnp.where(low_half, x0, x1))
             gap = [tuple((a - b) * scale for a, b in zip(mine[i], other[i])) for i in (0, 1)]
         place_rhs(rhs, face, 0, *gap[0])
@@ -323,40 +372,21 @@
     jvp[:, cols] = total[0:TERMS, 128:256]
 
 
-def kernel(pairs, ids, coefs, start, field, left, right, mass, source, res, jvp, rhs, kc, acc):
-    base = start[0]
+def kernel(
+    pairs, space_count, halo_depth, neighbors, field, left, right, mass, source, res, jvp, rhs,
+    kc, acc,
+):
+    base = lax.axis_index("chaos") * pairs
+    ranks = (lax.axis_index("space"), space_count, neighbors.shape[0])
 
     def body(pair, carry):
-        pair_work(pair, base, ids, coefs, field, left, right, mass, source, res, jvp, rhs, kc, acc, None)
+        pair_work(
+            pair, base, ranks, halo_depth, neighbors, field, left, right, mass, source, res,
+            jvp, rhs, kc, acc,
+        )
         return carry
 
     lax.fori_loop(0, pairs, body, 0)
-
-
-def aux_rows(k_ref, sensitivity, decay, material):
-    table = jnp.concatenate(
-        [jnp.log(k_ref)[:, None], sensitivity, -decay[:, None]], axis=1
-    ) * np.float32(LOG2E)
-    mine = material.reshape(-1, 2)
-    spread = jnp.repeat(mine, SITES, axis=1)[:, None, :]
-    out = jnp.zeros((mine.shape[0], 8, 128), F32)
-    for m in range(NMAT):
-        out = jnp.where(spread == m, table[m][None, :, None], out)
-    return out
-
-
-def slots(neighbors, space_rank, space_count, chaos_rank, own_blocks, halo_depth):
-    blocks = neighbors.shape[0]
-    mine = lax.dynamic_slice_in_dim(neighbors, chaos_rank * own_blocks, own_blocks, 0)
-    halo_ref = mine - blocks
-    distance = (space_rank - halo_ref // halo_depth) % space_count
-    order = jnp.where(
-        distance == 1, 0, jnp.where(distance == space_count - 1, 1, jnp.where(distance == 2, 2, 3))
-    )
-    ids = jnp.where(mine >= blocks, blocks + order * halo_depth + halo_ref % halo_depth, mine)
-    ids = jnp.maximum(ids, 0).reshape(-1)
-    coefs = jnp.where(mine >= 0, 0.25, 0.0).astype(F32).reshape(-1)
-    return ids, coefs
 
 
 def per_device(
@@ -364,15 +394,12 @@
     material, neighbors, send_list,
 ):
     space_count = lax.axis_size("space")
-    space_rank = lax.axis_index("space")
-    chaos_rank = lax.axis_index("chaos")
     cells = chaos_modes.shape[1]
     pairs = cells // 128
     halo_depth = send_list.shape[2]
     queue = nodes.shape[0]
     blocks = material.shape[0]
-    aux = aux_rows(k_ref, sensitivity, decay, material)
-    order_left, order_right = order_tables(nodes.shape[1])
+    far = pl.BlockSpec(memory_space=pl.ANY)
     vmem = pl.BlockSpec(memory_space=pltpu.VMEM)
     smem = pl.BlockSpec(memory_space=pltpu.SMEM)
     field, left, right, mass = pl.pallas_call(
@@ -383,31 +410,34 @@
             jax.ShapeDtypeStruct((176, queue), BF),
             jax.ShapeDtypeStruct((88, 1), F32),
         ],
-        in_specs=[smem] + [vmem] * 8,
+        in_specs=[smem] * 5 + [far] * 5,
         out_specs=[vmem] * 4,
         scratch_shapes=[
+            pltpu.VMEM((TERMS, cells), F32),
+            pltpu.VMEM((TERMS, cells), F32),
+            pltpu.VMEM((nodes.shape[1], queue), F32),
+            pltpu.VMEM((1, queue), F32),
+            pltpu.VMEM((8, 256), F32),
+            pltpu.VMEM((NMAT, 8, 128), F32),
             pltpu.VMEM((4, 176, 128), F32),
             pltpu.VMEM((4, 176, 128), F32),
             pltpu.SemaphoreType.DMA((16,)),
             pltpu.SemaphoreType.DMA((16,)),
             pltpu.SemaphoreType.DMA((4,)),
             pltpu.SemaphoreType.DMA((4,)),
+            pltpu.SemaphoreType.DMA((5,)),
         ],
         compiler_params=pltpu.CompilerParams(
             collective_id=0, has_side_effects=True, vmem_limit_bytes=32 * 1024 * 1024
         ),
     )(
-        send_list.reshape(-1), chaos_modes, newton_heading, aux, nodes, nodes.T,
-        weights[None, :], jnp.asarray(order_left), jnp.asarray(order_right),
-    )
-    ids, coefs = slots(
-        neighbors, space_rank, space_count, chaos_rank, cells // SITES, halo_depth
-    )
-    start = (chaos_rank * pairs).astype(jnp.int32).reshape(1)
+        send_list.reshape(-1), k_ref, sensitivity, decay, material, chaos_modes, newton_heading,
+        nodes.T, weights[None, :], jnp.asarray(order_codes(nodes.shape[1])),
+    )
     return pl.pallas_call(
-        functools.partial(kernel, pairs),
+        functools.partial(kernel, pairs, space_count, halo_depth),
         out_shape=[jax.ShapeDtypeStruct((TERMS, cells), F32)] * 2,
-        in_specs=[smem, smem, smem, vmem, vmem, vmem, vmem, vmem],
+        in_specs=[smem, vmem, vmem, vmem, vmem, vmem],
         out_specs=[vmem, vmem],
         scratch_shapes=[
             pltpu.VMEM((7, 256, 512), BF),
@@ -415,7 +445,7 @@
             pltpu.VMEM((2, 512, 128), F32),
         ],
         compiler_params=pltpu.CompilerParams(vmem_limit_bytes=48 * 1024 * 1024),
-    )(ids, coefs, start, field, left, right, mass, source[None, :])
+    )(neighbors, field, left, right, mass, source[None, :])
 
 
 def solution(mesh):

time: 64.8 us -> 61.6 us (0.951)
  other arithmetic: 3.73 us -> 0 us
  Pallas kernels: 50.1 us -> 51.5 us
    unnamed x16 -> x22, local copies, waits for them, and re-layouts: 7.15 us -> 8.92 us
    broadcast_in_dim x7 -> x0, local copies, waits for them, and re-layouts: 1.16 us -> none  [the longest x2 0.75 us: aux_rows(): jnp.log(k_ref)[:, None]]
    pallas_call x1, Pallas kernels: 13.2 us -> 14.2 us  [per_device(): pl.pallas_call(functools.partial(kernel, pairs, space_count, halo_depth),...]
    select_n x2 -> x0, other arithmetic: 0.87 us -> none  [the longest x1 0.76 us: slots(): coefs = jnp.where(mine >= 0, 0.25, 0.0).astype(F32).reshape(-1)]
    eq x8 -> x0, local copies, waits for them, and re-layouts: 0.81 us -> none  [aux_rows(): out = jnp.where(spread == m, table[m][None, :, None], out)]
    max x1 -> x0, other arithmetic: 0.78 us -> none  [slots(): ids = jnp.maximum(ids, 0).reshape(-1)]
    mul x1 -> x0, other arithmetic: 0.76 us -> none  [aux_rows(): jnp.concatenate([jnp.log(k_ref)[:, None], sensitivity, -decay[:, None]],...]
    neg x1 -> x0, other arithmetic: 0.66 us -> none  [aux_rows(): -decay[:, None]]
where the time goes in v2:
time: 61.6 us; the launch traced here: 61.2 us
  Pallas kernels  51.5 us (84%)
  local copies, waits for them, and re-layouts  9 us (15%)
  between operations  0.66 us (1%)
    pallas_call x1, Pallas kernels, per_device(): pl.pallas_call(functools.partial(gather_kernel, (space_count, lax.axis_si...  37.4 us
    pallas_call x1, Pallas kernels, per_device(): pl.pallas_call(functools.partial(kernel, pairs, space_count, halo_depth),...  14.2 us
    unnamed x22, local copies, waits for them, and re-layouts  8.92 us

profile of v2, /device:TPU:0, one launch (start us, length us, event | category | flops | bytes accessed | tf_op | source)
XLA Modules:
  0.0 61.2 jit_solution(10266811841723237659)
XLA Ops:
  0.6 0.8 %copy.16 = s32[1,8,2]{2,1,0:T(8,128)S(1)} copy(s32[1,8,2]{1,2,0:T(2,128)} %param.22) | data formatting | bytes 128 | tf_op args[10]
  1.4 0.1 reshape.7.picks
  1.5 0.8 %copy.17.neighbors = s32[64,4]{1,0:T(8,128)S(1)} copy(s32[64,4]{0,1:T(4,128)} %param.21) | data formatting | bytes 2048 | tf_op args[9]
  2.2 0.0 copy-start
  2.2 1.0 %copy-done = f32[84,1024]{1,0:T(8,128)S(1)} copy-done((f32[84,1024]{1,0:T(8,128)S(1)}, f32[84,1024]{1,0:T(8,128)}, u32[]{:S(2)}) %copy-start) | copy-done | bytes 344088
  3.2 0.0 copy-start.1
  3.2 1.0 %copy-done.1 = f32[84,1024]{1,0:T(8,128)S(1)} copy-done((f32[84,1024]{1,0:T(8,128)S(1)}, f32[84,1024]{1,0:T(8,128)}, u32[]{:S(2)}) %copy-start.1) | copy-done | bytes 344088
  4.2 0.0 copy-start.2
  4.2 0.7 %copy-done.2 = f32[512,6]{0,1:T(8,128)S(1)} copy-done((f32[512,6]{0,1:T(8,128)S(1)}, f32[512,6]{0,1:T(8,128)}, u32[]{:S(2)}) %copy-start.2) | copy-done | bytes 12312
  4.9 0.0 copy-start.3
  4.9 0.7 %copy-done.3 = f32[8,256]{1,0:T(8,128)S(1)} copy-done((f32[8,256]{1,0:T(8,128)S(1)}, f32[8,256]{1,0:T(8,128)}, u32[]{:S(2)}) %copy-start.3) | copy-done | bytes 8216
  5.6 0.0 copy-start.5
  5.6 0.7 %copy-done.5 = f32[4,6]{1,0:T(4,128)S(1)} copy-done((f32[4,6]{1,0:T(4,128)S(1)}, f32[4,6]{1,0:T(4,128)}, u32[]{:S(2)}) %copy-start.5) | copy-done | bytes 120
  6.3 0.0 copy-start.6
  6.3 0.7 %copy-done.6 = f32[512]{0:T(512)S(1)} copy-done((f32[512]{0:T(512)S(1)}, f32[512]{0:T(512)}, u32[]{:S(2)}) %copy-start.6) | copy-done | bytes 2072
  7.0 0.0 copy-start.7
  7.0 0.7 %copy-done.7 = f32[4]{0:T(128)S(1)} copy-done((f32[4]{0:T(128)S(1)}, f32[4]{0:T(128)}, u32[]{:S(2)}) %copy-start.7) | copy-done | bytes 40
  7.6 0.0 copy-start.8
  7.6 0.7 %copy-done.8 = f32[4]{0:T(128)S(1)} copy-done((f32[4]{0:T(128)S(1)}, f32[4]{0:T(128)}, u32[]{:S(2)}) %copy-start.8) | copy-done | bytes 40
  8.3 0.0 copy-start.9
  8.3 0.7 %copy-done.9 = s32[64]{0:T(128)S(1)} copy-done((s32[64]{0:T(128)S(1)}, s32[64]{0:T(128)}, u32[]{:S(2)}) %copy-start.9) | copy-done | bytes 280
  9.0 37.4 %shard_map.131 = (f32[36,176,128]{2,1,0:T(8,128)S(1)}, bf16[512,256]{1,0:T(8,128)(2,1)S(1)}, bf16[176,512]{1,0:T(8,128)(2,1)S(1)}, f32[88,1]{1,0:T(8,128)S(1)}) custom-call(s32[16]{0:T(128)S(1)} %reshape.7.picks, f32[4]{0:T(128)S(1)} %copy-done.7, f32[4,6]{1,0:T(4,128)S(1)} %copy-done.5, f32[4]{0:T(128)S(1)} %copy-done.8, s32[64]{0:T(128)S(1)} %copy-done.9, ...), custom_call_target="tpu_custom_call" | custom-call | tf_op jit(solution)/shard_map/pallas_call | solution.py:405
  46.3 0.0 copy-start.4
  46.3 0.7 %copy-done.4 = f32[1024]{0:T(1024)S(1)} copy-done((f32[1024]{0:T(1024)S(1)}, f32[1024]{0:T(1024)}, u32[]{:S(2)}) %copy-start.4) | copy-done | bytes 4120
  47.0 14.2 %shard_map.132 = (f32[84,1024]{1,0:T(8,128)}, f32[84,1024]{1,0:T(8,128)}) custom-call(s32[64,4]{1,0:T(8,128)S(1)} %copy.17.neighbors, f32[36,176,128]{2,1,0:T(8,128)S(1)} %get-tuple-element.6.field, bf16[512,256]{1,0:T(8,128)(2,1)S(1)} %get-tuple-element.7.left, bf16[176,512]{1,0:T(8,128)(2,1)S(1)} %get-tuple-element.8.right, ...), custom_call_target="tpu_custom_call" | custom-call | tf_op jit(solution)/shard_map/pallas_call | solution.py:437
Async XLA Ops:
  2.2 1.0 %copy-start = (f32[84,1024]{1,0:T(8,128)S(1)}, f32[84,1024]{1,0:T(8,128)}, u32[]{:S(2)}) copy-start(f32[84,1024]{1,0:T(8,128)} %modes_far.1) | copy-start | bytes 1032196
  3.2 1.0 %copy-start.1 = (f32[84,1024]{1,0:T(8,128)S(1)}, f32[84,1024]{1,0:T(8,128)}, u32[]{:S(2)}) copy-start(f32[84,1024]{1,0:T(8,128)} %heading_far.1) | copy-start | bytes 1032196
  4.2 0.7 %copy-start.2 = (f32[512,6]{0,1:T(8,128)S(1)}, f32[512,6]{0,1:T(8,128)}, u32[]{:S(2)}) copy-start(f32[512,6]{0,1:T(8,128)} %param.15) | copy-start | bytes 36868
  4.9 0.7 %copy-start.3 = (f32[8,256]{1,0:T(8,128)S(1)}, f32[8,256]{1,0:T(8,128)}, u32[]{:S(2)}) copy-start(f32[8,256]{1,0:T(8,128)} %constant.2.clone.codes_far) | copy-start | bytes 24580
  5.6 0.7 %copy-start.5 = (f32[4,6]{1,0:T(4,128)S(1)}, f32[4,6]{1,0:T(4,128)}, u32[]{:S(2)}) copy-start(f32[4,6]{1,0:T(4,128)} %sensitivity.1) | copy-start | bytes 292
  6.3 0.7 %copy-start.6 = (f32[512]{0:T(512)S(1)}, f32[512]{0:T(512)}, u32[]{:S(2)}) copy-start(f32[512]{0:T(512)} %param.16) | copy-start | bytes 6148
  7.0 0.7 %copy-start.7 = (f32[4]{0:T(128)S(1)}, f32[4]{0:T(128)}, u32[]{:S(2)}) copy-start(f32[4]{0:T(128)} %k_ref.1) | copy-start | bytes 52
  7.6 0.7 %copy-start.8 = (f32[4]{0:T(128)S(1)}, f32[4]{0:T(128)}, u32[]{:S(2)}) copy-start(f32[4]{0:T(128)} %decay.1) | copy-start | bytes 52
  8.3 0.7 %copy-start.9 = (s32[64]{0:T(128)S(1)}, s32[64]{0:T(128)}, u32[]{:S(2)}) copy-start(s32[64]{0:T(128)} %material.1) | copy-start | bytes 772
  46.3 0.7 %copy-start.4 = (f32[1024]{0:T(1024)S(1)}, f32[1024]{0:T(1024)}, u32[]{:S(2)}) copy-start(f32[1024]{0:T(1024)} %param.14) | copy-start | bytes 12292

commit v3 on v2

--- a/solution.py
+++ b/solution.py
@@ -145,7 +145,7 @@
     return peers
 
 
-def spread_modes(chaos_count, peers, chaos, pairs, field, send, recv, meanwhile):
+def spread_modes(chaos_count, peers, chaos, pairs, field, send, recv, meanwhile, early):
     def block(owner, first, count):
         return field.at[pl.ds(owner * pairs + first, count), 0:168]
 
@@ -175,6 +175,7 @@
             {"chaos": across},
         )
         over.start()
+        early()
         copies[2].wait_recv()
         copies[3].wait_recv()
         on.wait_recv()
@@ -189,6 +190,7 @@
     for copy in copies:
         copy.start()
     meanwhile()
+    early()
     for copy in copies:
         copy.wait_recv()
     return copies
@@ -210,13 +212,14 @@
     return copies
 
 
-def gather_kernel(
-    sizes, picks, k_ref, sensitivity, decay, material, modes_far, heading_far, nodes_far,
-    weights_far, codes_far, field, left, right, mass,
+def whole_kernel(
+    sizes, picks, k_ref, sensitivity, decay, material, neighbors, modes_far, heading_far,
+    nodes_far, weights_far, codes_far, source, res, jvp,
+    field, left, right, mass, rhs, kc, acc,
     modes, heading, nodes_t, weights, codes, table, out, inbox,
     send, recv, halo_send, halo_recv, near,
 ):
-    space_count, chaos_count, pairs = sizes
+    space_count, chaos_count, pairs, halo_depth = sizes
     space = lax.axis_index("space")
     chaos = lax.axis_index("chaos")
     blocks = material.shape[0]
@@ -236,9 +239,20 @@
         load.wait()
     pack_own(modes, heading, pairs, chaos * pairs, field)
     peers = greet(space_count, chaos_count, space, chaos)
+    base = chaos * pairs
+    ranks = (space, space_count, blocks)
+
+    def early():
+        def body(pair, carry):
+            pair_first(pair, base, field, left, rhs, kc, acc)
+            return carry
+
+        lax.fori_loop(0, pairs, body, 0)
+
     copies = spread_modes(
         chaos_count, peers, chaos, pairs, field, send, recv,
         lambda: fill_tables(nodes_t, weights, codes, left, right, mass),
+        early,
     )
     halo = send_halo(space_count, space, picks, field, out, inbox, halo_send, halo_recv)
     for copy in copies:
@@ -246,6 +260,15 @@
     for i, copy in enumerate(halo):
         copy.wait()
         field[blocks // 2 + i] = inbox[i]
+
+    def late(pair, carry):
+        pair_second(
+            pair, base, ranks, halo_depth, neighbors, field, left, right, mass, source, res,
+            jvp, rhs, kc, acc,
+        )
+        return carry
+
+    lax.fori_loop(0, pairs, late, 0)
 
 
 def place_rhs(rhs, face, field, main, tail):
@@ -297,23 +320,35 @@
     return index, jnp.where(entry >= 0, np.float32(0.25), np.float32(0.0))
 
 
-def pair_work(
-    pair, base, ranks, halo_depth, neighbors, field, left, right, mass, source, res, jvp, rhs,
-    kc, acc,
-):
+def face_sum(basis, rhs, face, conduct, change):
+    r = jnp.dot(basis, rhs[face], preferred_element_type=F32)
+    k = jnp.exp2(r[:, 256:384])
+    a = conduct + k
+    b = change + k * r[:, 384:512]
+    gap = r[:, 0:128]
+    return a * gap, b * gap + a * r[:, 128:256]
+
+
+def place_face(rhs, face, gap, other):
+    place_rhs(rhs, face, 0, *gap[0])
+    place_rhs(rhs, face, 1, *gap[1])
+    place_rhs(rhs, face, 2, *other[2])
+    place_rhs(rhs, face, 3, *other[3])
+
+
+def pair_first(pair, base, field, left, rhs, kc, acc):
     lane = lax.broadcasted_iota(jnp.int32, (1, 128), 1)
-    low_half = lane < 64
     height = lane % 64
     x = field[base + pair]
     mine = fields(x)
     place_rhs(rhs, 6, 0, *mine[2])
     place_rhs(rhs, 6, 1, *mine[3])
-    for face in range(6):
+    for face in range(2):
         if face == 0:
             scale = jnp.where(height == 63, 0.0, 0.5)
             other = [tuple(pltpu.roll(a, 127, 1) for a in f) for f in mine]
             gap = [tuple((a - b) * scale for a, b in zip(mine[i], other[i])) for i in (0, 1)]
-        elif face == 1:
+        else:
             scale = jnp.where(height == 0, 1.0, 0.5)
             bottom = height == 0
             other = [tuple(pltpu.roll(a, 1, 1) for a in f) for f in mine]
@@ -324,42 +359,48 @@
             other = [
                 tuple(jnp.where(bottom, a, b) for a, b in zip(mine[i], other[i])) for i in range(4)
             ]
-        else:
-            e0, c0 = slot(neighbors, 2 * (base + pair), face - 2, ranks, halo_depth)
-            e1, c1 = slot(neighbors, 2 * (base + pair) + 1, face - 2, ranks, halo_depth)
-            x0 = half_turn(field[e0 // 2], e0 % 2 == 1)
-            x1 = half_turn(field[e1 // 2], e1 % 2 == 0)
-            scale = jnp.where(low_half, c0, c1)
-            other = fields(jnp.where(low_half, x0, x1))
-            gap = [tuple((a - b) * scale for a, b in zip(mine[i], other[i])) for i in (0, 1)]
-        place_rhs(rhs, face, 0, *gap[0])
-        place_rhs(rhs, face, 1, *gap[1])
-        place_rhs(rhs, face, 2, *other[2])
-        place_rhs(rhs, face, 3, *other[3])
-    total = None
-    count = left.shape[0] // 512
-    for part in range(count):
+        place_face(rhs, face, gap, other)
+    for part in range(left.shape[0] // 512):
         rows = slice(part * 512, part * 512 + 512)
         basis = left[rows]
         r = jnp.dot(basis, rhs[6, :, 0:256], preferred_element_type=F32)
-        conduct = jnp.exp2(r[:, 0:128])
-        kc[0] = conduct
-        kc[1] = conduct * r[:, 128:256]
-        for face in range(6):
-            r = jnp.dot(basis, rhs[face], preferred_element_type=F32)
-            k = jnp.exp2(r[:, 256:384])
-            a = kc[0] + k
-            b = kc[1] + k * r[:, 384:512]
-            gap = r[:, 0:128]
-            bal = a * gap
-            step = b * gap + a * r[:, 128:256]
+        kc[pair, 0, rows] = jnp.exp2(r[:, 0:128])
+        kc[pair, 1, rows] = kc[pair, 0, rows] * r[:, 128:256]
+        for face in range(2):
+            bal, step = face_sum(basis, rhs, face, kc[pair, 0, rows], kc[pair, 1, rows])
             if face == 0:
-                acc[0] = bal
-                acc[1] = step
+                acc[pair, 0, rows] = bal
+                acc[pair, 1, rows] = step
             else:
-                acc[0] += bal
-                acc[1] += step
-        both = jnp.concatenate([acc[0], acc[1]], 1)
+                acc[pair, 0, rows] += bal
+                acc[pair, 1, rows] += step
+
+
+def pair_second(
+    pair, base, ranks, halo_depth, neighbors, field, left, right, mass, source, res, jvp, rhs,
+    kc, acc,
+):
+    lane = lax.broadcasted_iota(jnp.int32, (1, 128), 1)
+    low_half = lane < 64
+    mine = fields(field[base + pair])
+    for face in range(2, 6):
+        e0, c0 = slot(neighbors, 2 * (base + pair), face - 2, ranks, halo_depth)
+        e1, c1 = slot(neighbors, 2 * (base + pair) + 1, face - 2, ranks, halo_depth)
+        x0 = half_turn(field[e0 // 2], e0 % 2 == 1)
+        x1 = half_turn(field[e1 // 2], e1 % 2 == 0)
+        scale = jnp.where(low_half, c0, c1)
+        other = fields(jnp.where(low_half, x0, x1))
+        gap = [tuple((a - b) * scale for a, b in zip(mine[i], other[i])) for i in (0, 1)]
+        place_face(rhs, face, gap, other)
+    total = None
+    for part in range(left.shape[0] // 512):
+        rows = slice(part * 512, part * 512 + 512)
+        basis = left[rows]
+        for face in range(2, 6):
+            bal, step = face_sum(basis, rhs, face, kc[pair, 0, rows], kc[pair, 1, rows])
+            acc[pair, 0, rows] += bal
+            acc[pair, 1, rows] += step
+        both = jnp.concatenate([acc[pair, 0, rows], acc[pair, 1, rows]], 1)
         high = both.astype(BF)
         low = (both - high.astype(F32)).astype(BF)
         w = right[:, rows]
@@ -372,23 +413,6 @@
     jvp[:, cols] = total[0:TERMS, 128:256]
 
 
-def kernel(
-    pairs, space_count, halo_depth, neighbors, field, left, right, mass, source, res, jvp, rhs,
-    kc, acc,
-):
-    base = lax.axis_index("chaos") * pairs
-    ranks = (lax.axis_index("space"), space_count, neighbors.shape[0])
-
-    def body(pair, carry):
-        pair_work(
-            pair, base, ranks, halo_depth, neighbors, field, left, right, mass, source, res,
-            jvp, rhs, kc, acc,
-        )
-        return carry
-
-    lax.fori_loop(0, pairs, body, 0)
-
-
 def per_device(
     chaos_modes, newton_heading, source, nodes, weights, k_ref, sensitivity, decay,
     material, neighbors, send_list,
@@ -399,20 +423,24 @@
     halo_depth = send_list.shape[2]
     queue = nodes.shape[0]
     blocks = material.shape[0]
-    far = pl.BlockSpec(memory_space=pl.ANY)
+    far = pl.BlockSpec(memory_space=pltpu.HBM)
     vmem = pl.BlockSpec(memory_space=pltpu.VMEM)
     smem = pl.BlockSpec(memory_space=pltpu.SMEM)
-    field, left, right, mass = pl.pallas_call(
-        functools.partial(gather_kernel, (space_count, lax.axis_size("chaos"), pairs)),
-        out_shape=[
-            jax.ShapeDtypeStruct((blocks // 2 + 4, 176, 128), F32),
-            jax.ShapeDtypeStruct((queue, 256), BF),
-            jax.ShapeDtypeStruct((176, queue), BF),
-            jax.ShapeDtypeStruct((88, 1), F32),
-        ],
-        in_specs=[smem] * 5 + [far] * 5,
-        out_specs=[vmem] * 4,
+    return pl.pallas_call(
+        functools.partial(
+            whole_kernel, (space_count, lax.axis_size("chaos"), pairs, halo_depth)
+        ),
+        out_shape=[jax.ShapeDtypeStruct((TERMS, cells), F32)] * 2,
+        in_specs=[smem] * 6 + [far] * 5 + [vmem],
+        out_specs=[vmem] * 2,
         scratch_shapes=[
+            pltpu.VMEM((blocks // 2 + 4, 176, 128), F32),
+            pltpu.VMEM((queue, 256), BF),
+            pltpu.VMEM((176, queue), BF),
+            pltpu.VMEM((88, 1), F32),
+            pltpu.VMEM((7, 256, 512), BF),
+            pltpu.VMEM((pairs, 2, queue, 128), F32),
+            pltpu.VMEM((pairs, 2, queue, 128), F32),
             pltpu.VMEM((TERMS, cells), F32),
             pltpu.VMEM((TERMS, cells), F32),
             pltpu.VMEM((nodes.shape[1], queue), F32),
@@ -428,24 +456,13 @@
             pltpu.SemaphoreType.DMA((5,)),
         ],
         compiler_params=pltpu.CompilerParams(
-            collective_id=0, has_side_effects=True, vmem_limit_bytes=32 * 1024 * 1024
+            collective_id=0, has_side_effects=True, vmem_limit_bytes=48 * 1024 * 1024
         ),
     )(
-        send_list.reshape(-1), k_ref, sensitivity, decay, material, chaos_modes, newton_heading,
-        nodes.T, weights[None, :], jnp.asarray(order_codes(nodes.shape[1])),
-    )
-    return pl.pallas_call(
-        functools.partial(kernel, pairs, space_count, halo_depth),
-        out_shape=[jax.ShapeDtypeStruct((TERMS, cells), F32)] * 2,
-        in_specs=[smem, vmem, vmem, vmem, vmem, vmem],
-        out_specs=[vmem, vmem],
-        scratch_shapes=[
-            pltpu.VMEM((7, 256, 512), BF),
-            pltpu.VMEM((2, 512, 128), F32),
-            pltpu.VMEM((2, 512, 128), F32),
-        ],
-        compiler_params=pltpu.CompilerParams(vmem_limit_bytes=48 * 1024 * 1024),
-    )(neighbors, field, left, right, mass, source[None, :])
+        send_list.reshape(-1), k_ref, sensitivity, decay, material, neighbors, chaos_modes,
+        newton_heading, nodes.T, weights[None, :], jnp.asarray(order_codes(nodes.shape[1])),
+        source[None, :],
+    )
 
 
 def solution(mesh):

time: 61.6 us -> 53.9 us (0.88)
  Pallas kernels: 51.5 us -> 47.4 us
  local copies, waits for them, and re-layouts: 9 us -> 5.6 us
    pallas_call x2 -> x1, Pallas kernels: 51.5 us -> 47.4 us  [per_device(): pl.pallas_call(functools.partial(whole_kernel, (space_count, lax.axis_siz...]
    unnamed x22 -> x28, local copies, waits for them, and re-layouts: 8.92 us -> 5.52 us
where the time goes in v3:
time: 53.9 us; the launch traced here: 53.7 us
  Pallas kernels  47.4 us (88%)
  local copies, waits for them, and re-layouts  5.6 us (10%)
  between operations  0.69 us (1%)
    pallas_call x1, Pallas kernels, per_device(): pl.pallas_call(functools.partial(whole_kernel, (space_count, lax.axis_siz...  47.4 us
    unnamed x28, local copies, waits for them, and re-layouts  5.52 us

profile of v3, /device:TPU:0, one launch (start us, length us, event | category | flops | bytes accessed | tf_op | source)
XLA Modules:
  0.0 53.7 jit_solution(9573829417851803433)
XLA Ops:
  0.6 0.0 copy-start.11
  0.6 0.7 %copy-done.11 = s32[1,8,2]{1,2,0:T(2,128)S(1)} copy-done((s32[1,8,2]{1,2,0:T(2,128)S(1)}, s32[1,8,2]{1,2,0:T(2,128)}, u32[]{:S(2)}) %copy-start.11) | copy-done | bytes 88
  1.3 0.1 copy.16
  1.4 0.0 copy-start.10
  1.4 0.1 reshape.7.picks
  1.5 0.6 %copy-done.10 = s32[64,4]{0,1:T(4,128)S(1)} copy-done((s32[64,4]{0,1:T(4,128)S(1)}, s32[64,4]{0,1:T(4,128)}, u32[]{:S(2)}) %copy-start.10) | copy-done | bytes 1048
  2.1 0.0 copy-start.2
  2.1 0.0 copy-start.3
  2.1 0.0 copy-start.4
  2.1 0.0 copy-start.5
  2.1 0.0 copy-start.6
  2.1 0.0 copy-start.7
  2.1 0.0 copy-start.8
  2.1 0.0 copy-start.9
  2.1 0.1 copy.17.neighbors
  2.2 0.6 %copy-done.2 = f32[512,6]{0,1:T(8,128)S(1)} copy-done((f32[512,6]{0,1:T(8,128)S(1)}, f32[512,6]{0,1:T(8,128)}, u32[]{:S(2)}) %copy-start.2) | copy-done | bytes 12312
  2.8 0.0 copy-done.3
  2.8 0.0 copy-done.4
  2.8 0.0 copy-done.5
  2.8 0.0 copy-done.6
  2.8 0.0 copy-done.7
  2.8 0.0 copy-done.8
  2.8 0.0 copy-done.9
  2.8 0.0 copy-start
  2.8 1.0 %copy-done = f32[84,1024]{1,0:T(8,128)S(1)} copy-done((f32[84,1024]{1,0:T(8,128)S(1)}, f32[84,1024]{1,0:T(8,128)}, u32[]{:S(2)}) %copy-start) | copy-done | bytes 344088
  3.8 0.0 copy-start.1
  3.8 1.0 %copy-done.1 = f32[84,1024]{1,0:T(8,128)S(1)} copy-done((f32[84,1024]{1,0:T(8,128)S(1)}, f32[84,1024]{1,0:T(8,128)}, u32[]{:S(2)}) %copy-start.1) | copy-done | bytes 344088
  4.8 47.4 %shard_map.131 = (f32[84,1024]{1,0:T(8,128)S(1)}, f32[84,1024]{1,0:T(8,128)S(1)}) custom-call(s32[16]{0:T(128)S(1)} %reshape.7.picks, f32[4]{0:T(128)S(1)} %copy-done.7, f32[4,6]{1,0:T(4,128)S(1)} %copy-done.5, f32[4]{0:T(128)S(1)} %copy-done.8, s32[64]{0:T(128)S(1)} %copy-done.9, s32[64,4]{1,0:T(8,128)S(1)} %copy.17.neighbors, f32[84,1024]{1,0:T(8,128)S(1)} %copy-done, ...), custom_call_target="tpu_custom_call" | custom-call | tf_op jit(solution)/shard_map/pallas_call | solution.py:429
  52.2 0.7 %copy.20 = f32[84,1024]{1,0:T(8,128)} copy(f32[84,1024]{1,0:T(8,128)S(1)} %get-tuple-element.4) | data formatting | bytes 688128
  52.9 0.7 %copy.21 = f32[84,1024]{1,0:T(8,128)} copy(f32[84,1024]{1,0:T(8,128)S(1)} %get-tuple-element.5) | data formatting | bytes 688128
Async XLA Ops:
  0.6 0.7 %copy-start.11 = (s32[1,8,2]{1,2,0:T(2,128)S(1)}, s32[1,8,2]{1,2,0:T(2,128)}, u32[]{:S(2)}) copy-start(s32[1,8,2]{1,2,0:T(2,128)} %param.22) | copy-start | bytes 196
  1.4 0.7 %copy-start.10 = (s32[64,4]{0,1:T(4,128)S(1)}, s32[64,4]{0,1:T(4,128)}, u32[]{:S(2)}) copy-start(s32[64,4]{0,1:T(4,128)} %param.21) | copy-start | bytes 3076
  2.1 0.7 %copy-start.2 = (f32[512,6]{0,1:T(8,128)S(1)}, f32[512,6]{0,1:T(8,128)}, u32[]{:S(2)}) copy-start(f32[512,6]{0,1:T(8,128)} %param.15) | copy-start | bytes 36868
  2.1 0.7 %copy-start.3 = (f32[8,256]{1,0:T(8,128)S(1)}, f32[8,256]{1,0:T(8,128)}, u32[]{:S(2)}) copy-start(f32[8,256]{1,0:T(8,128)} %constant.2.clone.codes_far) | copy-start | bytes 24580
  2.1 0.7 %copy-start.4 = (f32[1024]{0:T(1024)S(1)}, f32[1024]{0:T(1024)}, u32[]{:S(2)}) copy-start(f32[1024]{0:T(1024)} %param.14) | copy-start | bytes 12292
  2.1 0.7 %copy-start.5 = (f32[4,6]{1,0:T(4,128)S(1)}, f32[4,6]{1,0:T(4,128)}, u32[]{:S(2)}) copy-start(f32[4,6]{1,0:T(4,128)} %sensitivity.1) | copy-start | bytes 292
  2.1 0.7 %copy-start.6 = (f32[512]{0:T(512)S(1)}, f32[512]{0:T(512)}, u32[]{:S(2)}) copy-start(f32[512]{0:T(512)} %param.16) | copy-start | bytes 6148
  2.1 0.7 %copy-start.7 = (f32[4]{0:T(128)S(1)}, f32[4]{0:T(128)}, u32[]{:S(2)}) copy-start(f32[4]{0:T(128)} %k_ref.1) | copy-start | bytes 52
  2.1 0.7 %copy-start.8 = (f32[4]{0:T(128)S(1)}, f32[4]{0:T(128)}, u32[]{:S(2)}) copy-start(f32[4]{0:T(128)} %decay.1) | copy-start | bytes 52
  2.1 0.7 %copy-start.9 = (s32[64]{0:T(128)S(1)}, s32[64]{0:T(128)}, u32[]{:S(2)}) copy-start(s32[64]{0:T(128)} %material.1) | copy-start | bytes 772
  2.8 1.0 %copy-start = (f32[84,1024]{1,0:T(8,128)S(1)}, f32[84,1024]{1,0:T(8,128)}, u32[]{:S(2)}) copy-start(f32[84,1024]{1,0:T(8,128)} %modes_far.1) | copy-start | bytes 1032196
  3.8 1.0 %copy-start.1 = (f32[84,1024]{1,0:T(8,128)S(1)}, f32[84,1024]{1,0:T(8,128)}, u32[]{:S(2)}) copy-start(f32[84,1024]{1,0:T(8,128)} %heading_far.1) | copy-start | bytes 1032196

commit v4 on v3

--- a/solution.py
+++ b/solution.py
@@ -308,7 +308,7 @@
 
 def slot(neighbors, block, face, ranks, halo_depth):
     space, space_count, blocks = ranks
-    entry = neighbors[block, face]
+    entry = neighbors[face, block]
     away = jnp.maximum(entry - blocks, 0)
     distance = (space - away // halo_depth + space_count) % space_count
     order = jnp.where(
@@ -456,10 +456,10 @@
             pltpu.SemaphoreType.DMA((5,)),
         ],
         compiler_params=pltpu.CompilerParams(
-            collective_id=0, has_side_effects=True, vmem_limit_bytes=48 * 1024 * 1024
+            collective_id=0, has_side_effects=True, vmem_limit_bytes=60 * 1024 * 1024
         ),
     )(
-        send_list.reshape(-1), k_ref, sensitivity, decay, material, neighbors, chaos_modes,
+        send_list.reshape(-1), k_ref, sensitivity, decay, material, neighbors.T, chaos_modes,
         newton_heading, nodes.T, weights[None, :], jnp.asarray(order_codes(nodes.shape[1])),
         source[None, :],
     )

time: 53.9 us -> 53.1 us (0.985)
  local copies, waits for them, and re-layouts: 5.6 us -> 3.88 us
  Pallas kernels: 47.4 us -> 48.4 us
    unnamed x28 -> x7, local copies, waits for them, and re-layouts: 5.52 us -> 3.29 us
    pallas_call x1, Pallas kernels: 47.4 us -> 48.4 us  [per_device(): pl.pallas_call(functools.partial(whole_kernel, (space_count, lax.axis_siz...]
where the time goes in v4:
time: 53.1 us; the launch traced here: 52.9 us
  Pallas kernels  48.4 us (91%)
  local copies, waits for them, and re-layouts  3.88 us (7%)
  between operations  0.66 us (1%)
    pallas_call x1, Pallas kernels, per_device(): pl.pallas_call(functools.partial(whole_kernel, (space_count, lax.axis_siz...  48.4 us
    unnamed x7, local copies, waits for them, and re-layouts  3.29 us

profile of v4, /device:TPU:0, one launch (start us, length us, event | category | flops | bytes accessed | tf_op | source)
XLA Modules:
  0.0 52.9 jit_solution(17285390493564367946)
XLA Ops:
  0.6 0.0 copy-start.1
  0.6 0.7 %copy-done.1 = s32[1,8,2]{1,2,0:T(2,128)S(1)} copy-done((s32[1,8,2]{1,2,0:T(2,128)S(1)}, s32[1,8,2]{1,2,0:T(2,128)}, u32[]{:S(2)}) %copy-start.1) | copy-done | bytes 88
  1.3 0.1 copy.15
  1.4 0.6 %reshape.7.picks = s32[16]{0:T(128)} reshape(s32[1,8,2]{2,1,0:T(8,128)S(1)} %copy.15) | data formatting | bytes 128 | tf_op jit(solution)/shard_map/reshape | solution.py:462
  2.0 48.4 %shard_map.131 = (f32[84,1024]{1,0:T(8,128)}, f32[84,1024]{1,0:T(8,128)}) custom-call(s32[16]{0:T(128)} %reshape.7.picks, f32[4]{0:T(128)} %k_ref.1, f32[4,6]{1,0:T(4,128)} %sensitivity.1, f32[4]{0:T(128)} %decay.1, s32[64]{0:T(128)} %material.1, s32[4,64]{1,0:T(4,128)} %bitcast.6, f32[84,1024]{1,0:T(8,128)} %modes_far.1, f32[84,1024]{1,0:T(8,128)} %heading_far.1, ...), custom_call_target="tpu_custom_call" | custom-call | tf_op jit(solution)/shard_map/pallas_call | solution.py:429
  50.4 0.0 copy-start
  50.4 1.8 %copy.18 = f32[84,1024]{1,0:T(8,128)} copy(f32[84,1024]{1,0:T(8,128)} %get-tuple-element.4) | data formatting | bytes 688128
  52.2 0.0 copy-done
  52.2 0.7 %copy.19 = f32[84,1024]{1,0:T(8,128)} copy(f32[84,1024]{1,0:T(8,128)S(1)} %copy-done) | data formatting | bytes 688128
Async XLA Ops:
  0.6 0.7 %copy-start.1 = (s32[1,8,2]{1,2,0:T(2,128)S(1)}, s32[1,8,2]{1,2,0:T(2,128)}, u32[]{:S(2)}) copy-start(s32[1,8,2]{1,2,0:T(2,128)} %param.22) | copy-start | bytes 196
  50.4 1.8 %copy-start = (f32[84,1024]{1,0:T(8,128)S(1)}, f32[84,1024]{1,0:T(8,128)}, u32[]{:S(2)}) copy-start(f32[84,1024]{1,0:T(8,128)} %get-tuple-element.5) | copy-start | bytes 1032196

commit v5 on v4

--- a/solution.py
+++ b/solution.py
@@ -141,8 +141,7 @@
             barrier, inc=1, device_id={"space": (space + offset + space_count) % space_count},
             device_id_type=pl.DeviceIdType.MESH,
         )
-    pl.semaphore_wait(barrier, len(peers) + len(OFFSETS))
-    return peers
+    return barrier, peers
 
 
 def spread_modes(chaos_count, peers, chaos, pairs, field, send, recv, meanwhile, early):
@@ -223,6 +222,7 @@
     space = lax.axis_index("space")
     chaos = lax.axis_index("chaos")
     blocks = material.shape[0]
+    barrier, peers = greet(space_count, chaos_count, space, chaos)
     loads = [
         pltpu.make_async_copy(a, b, near.at[i])
         for i, (a, b) in enumerate(
@@ -238,7 +238,7 @@
     for load in loads:
         load.wait()
     pack_own(modes, heading, pairs, chaos * pairs, field)
-    peers = greet(space_count, chaos_count, space, chaos)
+    pl.semaphore_wait(barrier, len(peers) + len(OFFSETS))
     base = chaos * pairs
     ranks = (space, space_count, blocks)
 

time: 53.1 us -> 52 us (0.979)
  Pallas kernels: 48.4 us -> 47.3 us
    pallas_call x1, Pallas kernels: 48.4 us -> 47.3 us  [per_device(): pl.pallas_call(functools.partial(whole_kernel, (space_count, lax.axis_siz...]
where the time goes in v5:
time: 52 us; the launch traced here: 51.8 us
  Pallas kernels  47.3 us (91%)
  local copies, waits for them, and re-layouts  3.88 us (7%)
  between operations  0.66 us (1%)
    pallas_call x1, Pallas kernels, per_device(): pl.pallas_call(functools.partial(whole_kernel, (space_count, lax.axis_siz...  47.3 us
    unnamed x7, local copies, waits for them, and re-layouts  3.29 us

profile of v5, /device:TPU:0, one launch (start us, length us, event | category | flops | bytes accessed | tf_op | source)
XLA Modules:
  0.0 51.8 jit_solution(15893238007433441543)
XLA Ops:
  0.6 0.0 copy-start.1
  0.6 0.7 %copy-done.1 = s32[1,8,2]{1,2,0:T(2,128)S(1)} copy-done((s32[1,8,2]{1,2,0:T(2,128)S(1)}, s32[1,8,2]{1,2,0:T(2,128)}, u32[]{:S(2)}) %copy-start.1) | copy-done | bytes 88
  1.3 0.1 copy.15
  1.4 0.6 %reshape.7.picks = s32[16]{0:T(128)} reshape(s32[1,8,2]{2,1,0:T(8,128)S(1)} %copy.15) | data formatting | bytes 128 | tf_op jit(solution)/shard_map/reshape | solution.py:462
  2.0 47.3 %shard_map.131 = (f32[84,1024]{1,0:T(8,128)}, f32[84,1024]{1,0:T(8,128)}) custom-call(s32[16]{0:T(128)} %reshape.7.picks, f32[4]{0:T(128)} %k_ref.1, f32[4,6]{1,0:T(4,128)} %sensitivity.1, f32[4]{0:T(128)} %decay.1, s32[64]{0:T(128)} %material.1, s32[4,64]{1,0:T(4,128)} %bitcast.6, f32[84,1024]{1,0:T(8,128)} %modes_far.1, f32[84,1024]{1,0:T(8,128)} %heading_far.1, ...), custom_call_target="tpu_custom_call" | custom-call | tf_op jit(solution)/shard_map/pallas_call | solution.py:429
  49.3 0.0 copy-start
  49.3 1.8 %copy.18 = f32[84,1024]{1,0:T(8,128)} copy(f32[84,1024]{1,0:T(8,128)} %get-tuple-element.4) | data formatting | bytes 688128
  51.1 0.0 copy-done
  51.1 0.7 %copy.19 = f32[84,1024]{1,0:T(8,128)} copy(f32[84,1024]{1,0:T(8,128)S(1)} %copy-done) | data formatting | bytes 688128
Async XLA Ops:
  0.6 0.7 %copy-start.1 = (s32[1,8,2]{1,2,0:T(2,128)S(1)}, s32[1,8,2]{1,2,0:T(2,128)}, u32[]{:S(2)}) copy-start(s32[1,8,2]{1,2,0:T(2,128)} %param.22) | copy-start | bytes 196
  49.3 1.8 %copy-start = (f32[84,1024]{1,0:T(8,128)S(1)}, f32[84,1024]{1,0:T(8,128)}, u32[]{:S(2)}) copy-start(f32[84,1024]{1,0:T(8,128)} %get-tuple-element.5) | copy-start | bytes 1032196
